TPU v7x, 128 devices: a whole 4x4x4 slice. The times are simulated.
128 devices in a mesh: face: 8 (over z_lo, x), tile: 16 (over z_hi, y, core).
Axes of the slice: x: 4, y: 4, z: 4 (z_hi: 2, z_lo: 2; z = z_hi * 2 + z_lo), core: 2. Of those that a mesh axis runs over, the one named last changes fastest.
Arguments:
- source: bfloat16 [8192, 16, 128], P(('face', 'tile')), may hold values from -6 to 6
- entry_block: int32 [16384], P(('face', 'tile')), may hold values from 0 to 16383, as said below
- entry_source: int32 [16384], P(('face', 'tile')), may hold values from 0 to 63
- entry_weight: bfloat16 [16384, 128, 128], P(('face', 'tile')), may hold values from -0.5 to 0.5
- lat_to_nested: int32 [16384], P(('face', 'tile')), may hold values from 0 to 16383, as said below
- face_links: int32 [8, 4, 3], replicated, may hold values from 0 to 7, as said below
- w_in: bfloat16 [16, 90], replicated, may hold values from -1.5 to 1.5
- b_in: float32 [90], replicated, may hold values from -3 to 3
- kernel: float32 [9, 90], replicated, may hold values from -2 to 2
- ln_gain: float32 [90], replicated, may hold values from 0.1 to 1.9
- ln_bias: float32 [90], replicated, may hold values from -3 to 3
- w_one: bfloat16 [90, 360], replicated, may hold values from -0.625 to 0.625
- b_one: float32 [360], replicated, may hold values from -3 to 3
- w_two: bfloat16 [360, 90], replicated, may hold values from -0.3125 to 0.3125
- b_two: float32 [90], replicated, may hold values from -3 to 3
- cotangent: bfloat16 [8, 90, 512, 512], P('face', None, 'tile'), may hold values from -6 to 6
Outputs:
- output: bfloat16 [8, 90, 512, 512], P('face', None, 'tile')
- grad_one: float32 [90, 360], replicated
- grad_two: float32 [360, 90], replicated
- grad_kernel: float32 [9, 90], replicated
Inputs may be any that keep to these rules, and one draw needn't show every extreme that they name: `entry_block`: blocks k * 128 to (k + 1) * 128 - 1 belong to device k. At most 2 entries of one device name blocks of one device; in every draw one device gets exactly 2 from every device. `lat_to_nested`: A permutation of all blocks; the 128 blocks of each device go one to each device. `face_links`: entry [f, s, 0] names a face other than f; [f, s, 1] a side 0 to 3; [f, s, 2] is 0 or 1.
All inputs are finite; a program needn't handle non-finite values.
Results may differ from a plain program's by a relative error of at most 0.0081.
Values may be sent and summed in bfloat16 or wider, within the bound.
A program may use at most 192 MiB of HBM per device.

v0:
```python
import math

import jax
import jax.numpy as jnp
from jax import lax
from jax.sharding import PartitionSpec as P

CAP = 2


GELU_K = 0.7978845608028654
GELU_C = 0.044715
NORM_EPS = 1e-06


def with_halo(cells, sides, width):
    for axis, dim in sides:
        count = lax.axis_size(axis)
        ends = count - 1
        head = lax.slice_in_dim(cells, 0, width, axis=dim)
        tail = lax.slice_in_dim(cells, cells.shape[dim] - width, cells.shape[dim], axis=dim)
        cells = jnp.concatenate(
            [
                lax.ppermute(tail, axis, [(i, (i + 1) % count) for i in range(ends)]),
                cells,
                lax.ppermute(head, axis, [((i + 1) % count, i) for i in range(ends)]),
            ],
            axis=dim,
        )
    return cells


def gelu_pair(pre_act):
    inner = GELU_K * (pre_act + GELU_C * pre_act * pre_act * pre_act)
    tanh_val = jnp.tanh(inner)
    gelu_val = 0.5 * pre_act * (1.0 + tanh_val)
    gelu_slope = 0.5 * (1.0 + tanh_val) + 0.5 * pre_act * (1.0 - tanh_val * tanh_val) * GELU_K * (
        1.0 + 3.0 * GELU_C * pre_act * pre_act
    )
    return (gelu_val, gelu_slope)


def contract_rows(left_mat, right_mat):
    return lax.dot_general(
        left_mat, right_mat, (((1,), (1,)), ((), ())), preferred_element_type=jnp.float32
    )


def strip_work(padded, middle, cotan, kernel, ln_gain, ln_bias, w_one, b_one, w_two, b_two, scale):
    lat_count = padded.shape[0]
    row_count = padded.shape[1] - 2
    col_count = padded.shape[2] - 2
    wide = padded.astype(jnp.float32)
    depth_sum = jnp.zeros((lat_count, row_count, col_count), jnp.float32)
    for tap_index in range(9):
        row_off = tap_index // 3
        col_off = tap_index % 3
        window = wide[:, row_off : row_off + row_count, col_off : col_off + col_count]
        depth_sum = depth_sum + kernel[tap_index][:, None, None] * window
    flat = depth_sum.reshape(lat_count, row_count * col_count)
    mean_val = jnp.mean(flat, axis=0, keepdims=True)
    centered = flat - mean_val
    variance = jnp.mean(centered * centered, axis=0, keepdims=True)
    inv_std = lax.rsqrt(variance + NORM_EPS)
    scaled = centered * inv_std
    normed = (scaled * ln_gain[:, None] + ln_bias[:, None]).astype(jnp.bfloat16)
    pre_act = jnp.dot(w_one.T, normed, preferred_element_type=jnp.float32) + b_one[:, None]
    gelu_val, gelu_slope = gelu_pair(pre_act)
    hidden = gelu_val.astype(jnp.bfloat16)
    summed = (
        jnp.dot(w_two.T, hidden, preferred_element_type=jnp.float32)
        + b_two[:, None]
        + middle.reshape(lat_count, -1).astype(jnp.float32)
    )
    output = summed.astype(jnp.bfloat16).reshape(lat_count, row_count, col_count)
    cot_flat = cotan.reshape(lat_count, -1)
    grad_two = contract_rows(hidden, cot_flat) * scale
    back_hidden = jnp.dot(w_two, cot_flat, preferred_element_type=jnp.float32)
    back_pre = (back_hidden * gelu_slope).astype(jnp.bfloat16)
    grad_one = contract_rows(normed, back_pre) * scale
    back_hat = jnp.dot(w_one, back_pre, preferred_element_type=jnp.float32) * ln_gain[:, None]
    back_depth = inv_std * (
        back_hat
        - jnp.mean(back_hat, axis=0, keepdims=True)
        - scaled * jnp.mean(back_hat * scaled, axis=0, keepdims=True)
    )
    back_grid = back_depth.reshape(lat_count, row_count, col_count)
    kernel_rows = []
    for tap_index in range(9):
        row_off = tap_index // 3
        col_off = tap_index % 3
        window = wide[:, row_off : row_off + row_count, col_off : col_off + col_count]
        kernel_rows.append(jnp.sum(back_grid * window, axis=(1, 2)))
    grad_kernel = jnp.stack(kernel_rows, axis=0) * scale
    return (output, grad_one, grad_two, grad_kernel)


def lift(w_in, b_in, values):
    flat = values.reshape(values.shape[0], -1)
    mixed = jnp.dot(w_in.T, flat, preferred_element_type=jnp.float32) + b_in[:, None]
    return mixed.astype(jnp.bfloat16).reshape((w_in.shape[1],) + values.shape[1:])


def assemble(rows_part, cols_part):
    tile_count = rows_part.shape[0]
    chan_count = rows_part.shape[1]
    left_line = cols_part[:, 0].transpose(1, 0, 2).reshape(chan_count, -1)
    right_line = cols_part[:, 1].transpose(1, 0, 2).reshape(chan_count, -1)
    return jnp.stack([rows_part[0], rows_part[tile_count - 1], left_line, right_line], axis=0)


def per_device(
    source,
    entry_block,
    entry_source,
    entry_weight,
    lat_to_nested,
    face_links,
    w_in,
    b_in,
    kernel,
    ln_gain,
    ln_bias,
    w_one,
    b_one,
    w_two,
    b_two,
    cotangent,
):
    tile_count = lax.axis_size("tile")
    tile_at = lax.axis_index("tile")
    face_at = lax.axis_index("face")
    face_count = lax.axis_size("face")
    dev_count = lax.axis_size(("face", "tile"))
    in_count = source.shape[1]
    block_len = entry_weight.shape[2]
    row_count = cotangent.shape[2]
    line_len = cotangent.shape[3]
    chosen = jnp.take(source, entry_source, axis=0)
    partials = jnp.einsum(
        "eis,esp->eip", chosen, entry_weight, preferred_element_type=jnp.float32
    ).astype(jnp.bfloat16)
    owner_dev = entry_block // dev_count
    local_block = entry_block % dev_count
    hit_table = (owner_dev[:, None] == jnp.arange(dev_count, dtype=jnp.int32)[None, :]).astype(
        jnp.int32
    )
    slot_rank = jnp.sum((jnp.cumsum(hit_table, axis=0) - 1) * hit_table, axis=1)
    outbox = (
        jnp.zeros((dev_count, CAP, in_count, block_len), jnp.bfloat16)
        .at[owner_dev, slot_rank]
        .set(partials)
    )
    labels = (
        jnp.full((dev_count, CAP), dev_count, jnp.int32).at[owner_dev, slot_rank].set(local_block)
    )
    received, got_labels = (
        lax.all_to_all(outbox, ("face", "tile"), split_axis=0, concat_axis=0, tiled=True),
        lax.all_to_all(labels, ("face", "tile"), split_axis=0, concat_axis=0, tiled=True),
    )
    lat_sum = jnp.zeros((dev_count, in_count, block_len), jnp.float32)
    lat_sum = lat_sum.at[got_labels.reshape(-1)].add(
        received.reshape(-1, in_count, block_len).astype(jnp.float32), mode="drop"
    )
    lat_field = lat_sum.astype(jnp.bfloat16)
    target_dev = lat_to_nested // dev_count
    target_spot = lat_to_nested % dev_count
    outgoing = jnp.zeros_like(lat_field).at[target_dev].set(lat_field)
    out_spots = jnp.zeros((dev_count,), jnp.int32).at[target_dev].set(target_spot)
    incoming, in_spots = (
        lax.all_to_all(outgoing, ("face", "tile"), split_axis=0, concat_axis=0, tiled=True),
        lax.all_to_all(out_spots, ("face", "tile"), split_axis=0, concat_axis=0, tiled=True),
    )
    placed = jnp.zeros_like(incoming).at[in_spots].set(incoming)
    inputs_tile = placed.transpose(1, 0, 2).reshape(in_count, row_count, line_len)
    latent = lift(w_in, b_in, inputs_tile)
    chan_count = latent.shape[0]
    row_start = tile_at * row_count
    edge_cols = jnp.stack([latent[:, :, 0], latent[:, :, line_len - 1]], axis=0)
    edge_row = jnp.where(tile_at == 0, latent[:, 0, :], latent[:, row_count - 1, :])
    rows_face, cols_face = (
        lax.all_gather(edge_row.reshape(-1), "tile", axis=0, tiled=True),
        lax.all_gather(edge_cols.reshape(-1), "tile", axis=0, tiled=True),
    )
    own_lines = assemble(
        rows_face.reshape(tile_count, chan_count, line_len),
        cols_face.reshape(tile_count, 2, chan_count, row_count),
    )
    all_lines = lax.all_gather(own_lines.reshape(-1), "face", axis=0, tiled=True).reshape(
        face_count, 4, chan_count, line_len
    )
    face_link = face_links[face_at]
    picked = all_lines[face_link[:, 0], face_link[:, 1]]
    picked = jnp.where(face_link[:, 2][:, None, None] == 1, picked[:, :, ::-1], picked)
    row_lines = picked[0:2]
    full_cols = jnp.pad(picked[2:4], ((0, 0), (0, 0), (1, 1)))
    side_cols = lax.dynamic_slice_in_dim(full_cols, row_start, row_count + 2, 2)
    rim = jnp.stack([latent[:, 0, :], latent[:, row_count - 1, :]], axis=1)
    extended = with_halo(rim, (("tile", 1),), 1)
    upper_row = extended[:, 0, :]
    lower_row = extended[:, 3, :]
    spot_ids = jnp.arange(row_count + 2, dtype=jnp.int32) + row_start - 1
    inside = (spot_ids >= 0) & (spot_ids < line_len)
    side_cols = jnp.where(inside[None, None, :], side_cols, jnp.zeros_like(side_cols))
    top_row = jnp.where(tile_at == 0, row_lines[0], upper_row)
    bottom_row = jnp.where(tile_at == tile_count - 1, row_lines[1], lower_row)
    middle = jnp.concatenate([top_row[:, None, :], latent, bottom_row[:, None, :]], axis=1)
    padded = jnp.concatenate([side_cols[0][:, :, None], middle, side_cols[1][:, :, None]], axis=2)
    scale = 1.0 / math.sqrt(face_count * line_len * line_len)
    output, grad_one, grad_two, grad_kernel = strip_work(
        padded, latent, cotangent[0], kernel, ln_gain, ln_bias, w_one, b_one, w_two, b_two, scale
    )
    grad_one, grad_two, grad_kernel = lax.psum((grad_one, grad_two, grad_kernel), ("face", "tile"))
    return (output[None], grad_one, grad_two, grad_kernel)


def solution(mesh):
    placed = (
        P(("face", "tile"), None, None),
        P(("face", "tile")),
        P(("face", "tile")),
        P(("face", "tile"), None, None),
        P(("face", "tile")),
        P(),
        P(),
        P(),
        P(),
        P(),
        P(),
        P(),
        P(),
        P(),
        P(),
        P("face", None, "tile", None),
    )
    return jax.shard_map(
        per_device,
        mesh=mesh,
        in_specs=placed,
        out_specs=(P("face", None, "tile", None), P(), P(), P()),
        check_vma=False,
    )
```

profile of v0, /device:TPU:1, one launch (start us, length us, event | category | flops | bytes accessed | tf_op | source)
XLA Modules:
  0.0 591.9 jit_solution(9418654939937501962)
XLA Ops:
  15.5 11.5 %all-to-all-start.1 = ((s32[128,1,2]{2,1,0:T(1,128)}), s32[128,1,2]{2,1,0:T(1,128)S(1)}, u32[]{:S(2)}, u32[]{:S(2)}) async-start(s32[128,1,2]{2,1,0:T(1,128)} %copy.79), calls=%async_computation.1 | async-start | bytes 131072 | tf_op jit(solution)/shard_map/all_to_all | solution.py:159
  33.0 13.3 %scatter_fusion.1 = bf16[128,2,16,128]{3,2,1,0:T(8,128)(2,1)} fusion(bf16[128,2,16,128]{3,2,1,0:T(8,128)(2,1)} %broadcast_in_dim.46, s32[128]{0:T(128)S(1)} %fusion.33, bf16[128,16,128]{2,1,0:T(8,128)(2,1)S(1)} %convolution_convert_fusion), kind=kCustom, calls=%fused_computation.4 | custom fusion | bytes 1573888 | tf_op jit(solution)/shard_map/scatter | solution.py:152
  46.2 9.8 %all-to-all-start.2 = ((bf16[128,2,16,128]{3,2,1,0:T(8,128)(2,1)}), bf16[128,2,16,128]{3,2,1,0:T(8,128)(2,1)S(1)}, u32[]{:S(2)}, u32[]{:S(2)}) async-start(bf16[128,2,16,128]{3,2,1,0:T(8,128)(2,1)} %scatter_fusion.1), calls=%async_computation.2 | async-start | bytes 2097152 | tf_op jit(solution)/shard_map/all_to_all | solution.py:158
  59.2 15.7 %all-to-all-done.2 = bf16[128,2,16,128]{3,2,1,0:T(8,128)(2,1)S(1)} async-done(((bf16[128,2,16,128]{3,2,1,0:T(8,128)(2,1)}), bf16[128,2,16,128]{3,2,1,0:T(8,128)(2,1)S(1)}, u32[]{:S(2)}, u32[]{:S(2)}) %all-to-all-start.2) | async-done | bytes 1048608 | tf_op jit(solution)/shard_map/all_to_all | solution.py:158
  79.8 9.2 %scatter_fusion.2 = f32[128,16,128]{2,1,0:T(8,128)S(1)} fusion(f32[128,16,128]{2,1,0:T(8,128)S(1)} %broadcast_in_dim.43, s32[256]{0:T(256)S(1)} %bitcast.183, f32[256,16,128]{2,1,0:T(8,128)S(1)} %bitcast_convert_fusion), kind=kCustom, calls=%fused_computation.5 | custom fusion | flops 524288 | bytes 6292480 | tf_op jit(solution)/shard_map/scatter-add | solution.py:162
  89.9 13.2 %scatter_fusion.3 = bf16[128,16,128]{2,1,0:T(8,128)(2,1)} fusion(bf16[128,16,128]{2,1,0:T(8,128)(2,1)} %broadcast.194.clone, s32[128]{0:T(128)S(1)} %get-tuple-element.46, bf16[128,16,128]{2,1,0:T(8,128)(2,1)S(1)} %convert_element_type.45), kind=kCustom, calls=%fused_computation.6 | custom fusion | bytes 1573376 | tf_op jit(solution)/shard_map/scatter | solution.py:168
  103.1 9.9 %all-to-all-start.3 = ((bf16[128,16,128]{2,1,0:T(8,128)(2,1)}), bf16[128,16,128]{2,1,0:T(8,128)(2,1)S(1)}, u32[]{:S(2)}, u32[]{:S(2)}) async-start(bf16[128,16,128]{2,1,0:T(8,128)(2,1)} %scatter_fusion.3), calls=%async_computation.3 | async-start | bytes 1048576 | tf_op jit(solution)/shard_map/all_to_all | solution.py:171
  115.9 10.7 %all-to-all-done.3 = bf16[128,16,128]{2,1,0:T(8,128)(2,1)S(1)} async-done(((bf16[128,16,128]{2,1,0:T(8,128)(2,1)}), bf16[128,16,128]{2,1,0:T(8,128)(2,1)S(1)}, u32[]{:S(2)}, u32[]{:S(2)}) %all-to-all-start.3) | async-done | bytes 524320 | tf_op jit(solution)/shard_map/all_to_all | solution.py:171
  127.4 13.2 %scatter_fusion.4 = bf16[128,16,128]{2,1,0:T(8,128)(2,1)} fusion(bf16[128,16,128]{2,1,0:T(8,128)(2,1)} %broadcast.194, s32[128]{0:T(128)S(1)} %fusion.31, bf16[128,16,128]{2,1,0:T(8,128)(2,1)S(1)} %all-to-all-done.3), kind=kCustom, calls=%fused_computation.7 | custom fusion | bytes 1573376 | tf_op jit(solution)/shard_map/scatter | solution.py:174
  154.1 23.3 %all-gather = bf16[16,1,5760]{2,1,0:T(2,128)(2,1)} all-gather(bf16[1,1,5760]{2,1,0:T(2,128)(2,1)S(1)} %reshape.282), channel_id=1, replica_groups=mesh['face'=8,'tile'=16] {'tile'}, dimensions={0}, use_global_device_ids=true | all-gather | bytes 195840 | tf_op jit(solution)/shard_map/all_gather | solution.py:183
  214.0 24.0 %all-gather.6.cloned.1.call-done = bf16[1474560]{0:T(1024)(128)(2,1)} async-done(((bf16[184320]{0:T(1024)(128)(2,1)}), bf16[1474560]{0:T(1024)(128)(2,1)}) %all-gather.6.cloned.1.call-update) | async-done | bytes 2949136 | tf_op jit(solution)/shard_map/all_gather | solution.py:189
  246.9 8.5 %rev.3 = bf16[4,90,512]{2,1,0:T(8,128)(2,1)} reverse(bf16[4,90,512]{2,1,0:T(8,128)(2,1)} %gather_fusion.1), dimensions={2} | reverse | bytes 737280 | tf_op jit(solution)/shard_map/rev | solution.py:194
  262.7 8.9 %maximum_convert_fusion = f32[90,34,514]{2,1,0:T(8,128)} fusion(bf16[90,34,1]{2,1,0:T(8,128)(2,1)} %copy.94, bf16[90,1,512]{2,1,0:T(2,128)(2,1)S(1)} %copy.91, bf16[90,32,512]{2,1,0:T(8,128)(2,1)} %slice.204, bf16[90,1,512]{2,1,0:T(2,128)(2,1)} %copy.90, bf16[90,34,1]{2,1,0:T(8,128)(2,1)} %copy.93), kind=kLoop, calls=%fused_computation.45 | loop fusion | flops 15728400 | bytes 9437040 | tf_op jit(solution)/shard_map/convert_element_type | solution.py:53
  271.7 34.9 %fusion.38 = (f32[32,512]{1,0:T(8,128)S(1)}, f32[90,32,512]{2,1,0:T(8,128)}) fusion(f32[90,34,514]{2,1,0:T(8,128)} %maximum_convert_fusion, f32[90]{0:T(128)S(1)} %get-tuple-element.41, f32[90]{0:T(128)S(1)} %get-tuple-element.42, f32[90]{0:T(128)S(1)} %get-tuple-element.35, f32[90]{0:T(128)S(1)} %get-tuple-element.36, f32[90]{0:T(128)S(1)} %get-tuple-element.37, ...), kind=kLoop, calls=%fused_computation.128 | loop fusion | flops 26525696 | bytes 59051176 | tf_op jit(solution)/shard_map/reduce_sum | solution.py:61
  315.5 15.2 %multiply_convert_fusion = (bf16[360,16384]{1,0:T(8,128)(2,1)}, f32[16384,360]{0,1:T(8,128)}) fusion(f32[360]{0:T(512)S(1)} %copy-done.16, bf16[90,360]{1,0:T(8,128)(2,1)S(1)} %copy-done.7, f32[90,16384]{1,0:T(8,128)S(1)} %bitcast.150, f32[90]{0:T(128)S(1)} %copy-done.15, f32[90]{0:T(128)S(1)} %copy-done.10, f32[16384]{0:T(1024)S(1)} %bitcast.169, ...), kind=kOutput, calls=%fused_computation.18 | convolution fusion | flops 1128038400 | bytes 41485712 | tf_op jit(solution)/shard_map/dot_general | solution.py:67
  330.7 20.6 %fusion.6 = bf16[360,16384]{1,0:T(8,128)(2,1)} fusion(f32[16384,360]{0,1:T(8,128)} %get-tuple-element.48, bf16[360,90]{0,1:T(8,128)(2,1)S(1)} %copy-done.8, bf16[90,16384]{1,0:T(8,128)(2,1)S(1)} %bitcast.165), kind=kOutput, calls=%fused_computation.16 | convolution fusion | flops 1173749760 | bytes 38403360 | tf_op jit(solution)/shard_map/dot_general | solution.py:78
  351.3 8.7 %convolution_multiply_fusion.1 = f32[90,360]{1,0:T(8,128)} fusion(bf16[360,16384]{1,0:T(8,128)(2,1)} %fusion.6, f32[90,16384]{1,0:T(8,128)S(1)} %bitcast.151, f32[90]{0:T(128)S(1)} %copy-done.15, f32[90]{0:T(128)S(1)} %copy-done.10, f32[16384]{0:T(1024)S(1)} %bitcast.170, f32[16384]{0:T(1024)S(1)} %bitcast.174), kind=kOutput, calls=%fused_computation.48 | convolution fusion | flops 1069088384 | bytes 17956112 | tf_op jit(solution)/shard_map/dot_general | solution.py:44
  360.0 10.5 %fusion.13 = (f32[16384]{0:T(1024)S(1)}, f32[16384,90]{0,1:T(8,128)}) fusion(f32[90,16384]{1,0:T(8,128)S(1)} %bitcast.152, f32[16384]{0:T(1024)S(1)} %bitcast.171, f32[16384]{0:T(1024)S(1)} %bitcast.175, f32[90]{0:T(128)S(1)} %copy-done.10, bf16[360,16384]{1,0:T(8,128)(2,1)} %fusion.6, bf16[90,360]{1,0:T(8,128)(2,1)S(1)} %copy-done.7), kind=kOutput, calls=%fused_computation.31 | convolution fusion | flops 1069039616 | bytes 23854728 | tf_op jit(solution)/shard_map/dot_general | solution.py:81
  370.6 8.6 %convolution_multiply_fusion.2 = f32[360,90]{0,1:T(8,128)} fusion(bf16[360,16384]{1,0:T(8,128)(2,1)} %get-tuple-element.47, bf16[90,16384]{1,0:T(8,128)(2,1)S(1)} %bitcast.166), kind=kOutput, calls=%fused_computation.49 | convolution fusion | flops 1061715584 | bytes 14875200 | tf_op jit(solution)/shard_map/dot_general | solution.py:44
  379.1 6.9 %fusion.10 = bf16[90,16384]{1,0:T(8,128)(2,1)S(1)} fusion(bf16[360,16384]{1,0:T(8,128)(2,1)} %get-tuple-element.47, bf16[360,90]{0,1:T(8,128)(2,1)S(1)} %copy-done.8, bf16[16384,90]{0,1:T(8,128)(2,1)S(1)} %fusion.7, f32[90]{0:T(128)S(1)} %copy-done.11), kind=kOutput, calls=%fused_computation.26 | convolution fusion | flops 1067581440 | bytes 17759880 | tf_op jit(solution)/shard_map/dot_general | solution.py:71
  398.9 7.0 %copy.108 = f32[12,8,32,512]{3,2,1,0:T(8,128)} copy(f32[12,8,32,512]{3,1,2,0:T(8,128)S(1)} %bitcast.158) | data formatting | bytes 12582912
  405.9 31.9 %multiply_reduce_fusion = (f32[90]{0:T(128)S(1)}, f32[90]{0:T(128)S(1)}, f32[90]{0:T(128)S(1)}, f32[90]{0:T(128)S(1)}, f32[90]{0:T(128)S(1)}, /*index=5*/f32[90]...) fusion(f32[90,34,514]{2,1,0:T(8,128)} %maximum_convert_fusion, f32[96,32,512]{2,1,0:T(8,128)} %bitcast.159), kind=kLoop, calls=%fused_computation.34 | loop fusion | flops 26541270 | bytes 58985640 | tf_op jit(solution)/shard_map/reduce_sum | solution.py:93
  437.9 67.0 %psum.23 = f32[9,90]{1,0:T(8,128)} all-reduce(f32[9,90]{1,0:T(8,128)S(1)} %broadcast_multiply_fusion.3), channel_id=1, replica_groups=mesh['face'=8,'tile'=16] {'face','tile'}, use_global_device_ids=true, to_apply=%region_23.24 | all-reduce | flops 810 | bytes 6480 | tf_op jit(solution)/shard_map/psum | solution.py:213
  504.8 77.2 %all-reduce.4.cloned.1.call-done = (f32[90,360]{1,0:T(8,128)}, f32[360,90]{0,1:T(8,128)}) async-done(((f32[90,360]{1,0:T(8,128)}, f32[360,90]{0,1:T(8,128)}), (f32[90,360]{1,0:T(8,128)}, f32[360,90]{0,1:T(8,128)})) %all-reduce.4.cloned.1.call-update) | async-done | bytes 259216 | tf_op jit(solution)/shard_map/psum | solution.py:213
  (142 shorter events, 117.9 us)
Async XLA Ops:
  7.2 20.5 %copy-start = (bf16[64,16,128]{2,1,0:T(8,128)(2,1)S(1)}, bf16[64,16,128]{2,1,0:T(8,128)(2,1)}, u32[]{:S(2)}) copy-start(bf16[64,16,128]{2,1,0:T(8,128)(2,1)} %param.16) | copy-start | bytes 786436
  8.0 48.0 %copy-start.17 = (s32[128]{0:T(128)S(1)}, s32[128]{0:T(128)}, u32[]{:S(2)}) copy-start(s32[128]{0:T(128)} %param.20) | copy-start | bytes 1540
  15.5 30.7 %all-to-all-start.1 = ((s32[128,1,2]{2,1,0:T(1,128)}), s32[128,1,2]{2,1,0:T(1,128)S(1)}, u32[]{:S(2)}, u32[]{:S(2)}) async-start(s32[128,1,2]{2,1,0:T(1,128)} %copy.79), calls=%async_computation.1 | async-start | bytes 131072 | tf_op jit(solution)/shard_map/all_to_all | solution.py:159
  46.2 28.7 %all-to-all-start.2 = ((bf16[128,2,16,128]{3,2,1,0:T(8,128)(2,1)}), bf16[128,2,16,128]{3,2,1,0:T(8,128)(2,1)S(1)}, u32[]{:S(2)}, u32[]{:S(2)}) async-start(bf16[128,2,16,128]{3,2,1,0:T(8,128)(2,1)} %scatter_fusion.1), calls=%async_computation.2 | async-start | bytes 2097152 | tf_op jit(solution)/shard_map/all_to_all | solution.py:158
  74.9 28.2 %all-to-all-start = ((s32[128,1,1]{2,1,0:T(1,128)}), s32[128,1,1]{2,1,0:T(1,128)S(1)}, u32[]{:S(2)}, u32[]{:S(2)}) async-start(s32[128,1,1]{2,1,0:T(1,128)} %copy.78), calls=%async_computation | async-start | bytes 131072 | tf_op jit(solution)/shard_map/all_to_all | solution.py:172
  79.8 60.9 %copy-start.12 = (bf16[16,90]{1,0:T(8,128)(2,1)S(1)}, bf16[16,90]{1,0:T(8,128)(2,1)}, u32[]{:S(2)}) copy-start(bf16[16,90]{1,0:T(8,128)(2,1)} %param.22) | copy-start | bytes 8644
  79.8 60.8 %copy-start.14 = (f32[90]{0:T(128)S(1)}, f32[90]{0:T(128)}, u32[]{:S(2)}) copy-start(f32[90]{0:T(128)} %param.23) | copy-start | bytes 1084
  103.1 23.5 %all-to-all-start.3 = ((bf16[128,16,128]{2,1,0:T(8,128)(2,1)}), bf16[128,16,128]{2,1,0:T(8,128)(2,1)S(1)}, u32[]{:S(2)}, u32[]{:S(2)}) async-start(bf16[128,16,128]{2,1,0:T(8,128)(2,1)} %scatter_fusion.3), calls=%async_computation.3 | async-start | bytes 1048576 | tf_op jit(solution)/shard_map/all_to_all | solution.py:171
  113.0 77.5 %all-gather.4.cloned.1.call-start = ((), (), s32[]{:S(2)}) async-start(), calls=%async_computation.4 | async-start | bytes 1566720 | tf_op jit(solution)/shard_map/all_gather | solution.py:182
  143.9 1.7 copy-start.3
  146.6 52.0 %copy-start.9 = (s32[8,4,3]{0,1,2:T(4,128)S(1)}, s32[8,4,3]{0,1,2:T(4,128)}, u32[]{:S(2)}) copy-start(s32[8,4,3]{0,1,2:T(4,128)} %param.21) | copy-start | bytes 1156
  147.3 90.7 %all-gather.6.cloned.1.call-start = ((), (), s32[]{:S(2)}) async-start(), calls=%async_computation.5 | async-start | bytes 3317760 | tf_op jit(solution)/shard_map/all_gather | solution.py:189
  198.3 6.8 %copy-start.13 = (f32[9,90]{1,0:T(8,128)S(1)}, f32[9,90]{1,0:T(8,128)}, u32[]{:S(2)}) copy-start(f32[9,90]{1,0:T(8,128)} %param.24) | copy-start | bytes 9724
  198.3 383.7 %all-reduce.4.cloned.1.call-start = ((), (), s32[]{:S(2)}) async-start(), calls=%async_computation.6 | async-start | bytes 589824 | tf_op jit(solution)/shard_map/psum | solution.py:213
  209.0 50.1 %collective-permute-start = (bf16[90,1,512]{2,0,1:T(8,128)(2,1)}, bf16[90,1,512]{2,0,1:T(8,128)(2,1)S(1)}, u32[]{:S(2)}, u32[]{:S(2)}) collective-permute-start(bf16[90,1,512]{2,0,1:T(8,128)(2,1)} %get-tuple-element.18), channel_id=1, source_target_pairs={{0,1},{1,2},{2,3},{3,4},{4,5},{5,6},{6,7},{7,8},{8,9},{9,10},{10,1... | collective-permute-start | bytes 276488 | tf_op jit(solution)/shard_map/ppermute | solution.py:24
  212.1 47.1 %collective-permute-start.1 = (bf16[90,1,512]{2,0,1:T(8,128)(2,1)}, bf16[90,1,512]{2,0,1:T(8,128)(2,1)}, u32[]{:S(2)}, u32[]{:S(2)}) collective-permute-start(bf16[90,1,512]{2,0,1:T(8,128)(2,1)} %get-tuple-element.19), channel_id=1, source_target_pairs={{1,0},{2,1},{3,2},{4,3},{5,4},{6,5},{7,6},{8,7},{9,8},{10,9},{11,1... | collective-permute-start | bytes 276488 | tf_op jit(solution)/shard_map/ppermute | solution.py:26
  306.6 8.0 %slice-start = ((s8[5898240]{0:T(1024)(128)(4,1)}), s8[4194304]{0:T(1024)(128)(4,1)S(1)}, s32[]{:S(2)}) async-start(s8[5898240]{0:T(1024)(128)(4,1)} %bitcast.154), calls=%async_computation.7 | async-start | bytes 8388608
  310.1 4.5 slice-start.1
  314.5 45.5 %copy-start.2 = (f32[12,8,32,512]{3,1,2,0:T(8,128)}, f32[12,8,32,512]{3,1,2,0:T(8,128)S(1)}, u32[]{:S(2)}) copy-start(f32[12,8,32,512]{3,1,2,0:T(8,128)S(1)} %copy.103) | copy-start | bytes 18874372
  315.5 15.2 %copy-start.4 = (bf16[12,8,32,512]{3,1,2,0:T(8,128)(2,1)S(1)}, bf16[12,8,32,512]{3,1,2,0:T(8,128)(2,1)}, u32[]{:S(2)}) copy-start(bf16[12,8,32,512]{3,1,2,0:T(8,128)(2,1)} %copy.107) | copy-start | bytes 9437188
  315.5 15.2 %copy-start.8 = (bf16[360,90]{0,1:T(8,128)(2,1)S(1)}, bf16[360,90]{0,1:T(8,128)(2,1)}, u32[]{:S(2)}) copy-start(bf16[360,90]{0,1:T(8,128)(2,1)} %param.29) | copy-start | bytes 194404
  360.0 10.6 %copy-start.5 = (bf16[12,8,32,512]{3,1,2,0:T(8,128)(2,1)S(1)}, bf16[12,8,32,512]{3,1,2,0:T(8,128)(2,1)}, u32[]{:S(2)}) copy-start(bf16[12,8,32,512]{3,1,2,0:T(8,128)(2,1)} %copy.107) | copy-start | bytes 9437188
  370.6 8.6 %copy-start.11 = (f32[90]{0:T(128)S(1)}, f32[90]{0:T(128)}, u32[]{:S(2)}) copy-start(f32[90]{0:T(128)} %param.30) | copy-start | bytes 1084
  405.9 179.3 %copy-start.1 = (bf16[64,16,128]{2,1,0:T(8,128)(2,1)S(1)}, bf16[64,16,128]{2,1,0:T(8,128)(2,1)}, u32[]{:S(2)}) copy-start(bf16[64,16,128]{2,1,0:T(8,128)(2,1)} %param.16) | copy-start | bytes 786436
  (5 other events, 4.5 us)
Sparse Core Ops, SparseCore 0:
  147.4 43.0 all-gather.3
  198.4 39.5 all-gather.5
  437.9 144.0 all-reduce.3
where the time goes:
time: 601 us; the launch traced here: 592 us
  waiting for transfers between devices  132 us (22%)
  local copies, waits for them, and re-layouts  130 us (22%)
  other arithmetic  107 us (18%)
  blocking collectives  90.3 us (15%)
  matrix products  76 us (13%)
  starting transfers between devices  41.4 us (7%)
  between operations  14.6 us (2%)
    psum x1, waiting for transfers between devices, per_device(): lax.psum((grad_one, grad_two, grad_kernel), ('face', 'tile'))  77.2 us
    psum x1, blocking collectives, per_device(): lax.psum((grad_one, grad_two, grad_kernel), ('face', 'tile'))  67 us
    reduce_sum x1, other arithmetic, strip_work(): mean_val = jnp.mean(flat, axis=0, keepdims=True)  34.9 us
    unnamed x54, local copies, waits for them, and re-layouts  33.3 us
    reduce_sum x1, other arithmetic, strip_work(): kernel_rows.append(jnp.sum(back_grid * window, axis=(1, 2)))  31.9 us
    all_gather x1, waiting for transfers between devices, per_device(): lax.all_gather(own_lines.reshape(-1), 'face', axis=0, tiled=True)  24 us
    all_gather x1, blocking collectives, per_device(): lax.all_gather(edge_cols.reshape(-1), 'tile', axis=0, tiled=True)  23.3 us
    dot_general x1, matrix products, strip_work(): back_hidden = jnp.dot(w_two, cot_flat, preferred_element_type=jnp.float32)  20.6 us
  transfers between devices with their start and end apart: 9, of which 5 were waited for; matrix products, arithmetic and copies ran while one was open for 16% of the time, Pallas kernels for 0%

commit v1 on v0

v1 whole, which is shorter than its diff:
```python
import functools
import math

import jax
import jax.numpy as jnp
from jax import lax
from jax.experimental import pallas as pl
from jax.experimental.pallas import tpu as pltpu
from jax.sharding import PartitionSpec as P


GELU_K = 0.7978845608028654
GELU_C = 0.044715
NORM_EPS = 1e-06
CP = 96
HP = 368
UNROLL = 2
MIB = 1024 * 1024


def strip_kernel(
    inv_ref, flag_ref, blocks_ref, rows_ref, cols_ref, cot_ref, win_ref, vec_ref, kern_ref, w1t_ref, w2t_ref, w1_ref,
    w2_ref, out_ref, grad_ref, field, cols, cot_s, out_s, depth_s, scaled_s, norm_s, cotb_s, pre_s, back_s, hid_s, bp_s,
    bd_s, g2_s, g1_s, gk_s, scale,
):
    chans, rows, width = cot_ref.shape
    lanes = width // 128
    f32 = jnp.float32
    bf16 = jnp.bfloat16

    def wide(v):
        return jnp.concatenate([v] * lanes, axis=1)

    def lift(x):
        return (jnp.dot(win_ref[...], x, preferred_element_type=f32)).astype(bf16)

    b_in = vec_ref[0]
    lane = lax.broadcasted_iota(jnp.int32, (CP, 128), 1)
    last = lane == jnp.where(flag_ref[1] == 1, rows + 1, -1)
    first = lane == jnp.where(flag_ref[0] == 1, 0, -1)
    for side in range(2):
        v = jnp.dot(win_ref[...], cols_ref[side], preferred_element_type=f32) + b_in
        v = v.astype(bf16).astype(f32)
        cols[side] = jnp.where(first | last, 0.0, v)

    g2_s[...] = jnp.zeros_like(g2_s)
    g1_s[...] = jnp.zeros_like(g1_s)
    gk_s[...] = jnp.zeros_like(gk_s)
    cot_s[:, chans * rows :, :] = jnp.zeros((lanes, (CP - chans) * rows, 128), f32)

    def turn(c, _):
        x = cot_ref[c].astype(f32)
        for k in range(lanes):
            cot_s[k, pl.ds(pl.multiple_of(c * rows, rows), rows), :] = x[:, k * 128 : (k + 1) * 128]
        return 0

    lax.fori_loop(0, chans, turn, 0)

    def make_row(at, x):
        lat = jnp.dot(win_ref[...], x, preferred_element_type=f32) + wide(b_in)
        lat = lat.astype(bf16).astype(f32)
        wide_lane = lax.broadcasted_iota(jnp.int32, (CP, width), 1)
        left = wide(pltpu.roll(cols[0], lax.rem(128 - at, 128), 1))
        right = wide(pltpu.roll(cols[1], 127 - at, 1))
        field[at, 0] = jnp.where(wide_lane == 0, left, pltpu.roll(lat, 1, 1))
        field[at, 1] = lat
        field[at, 2] = jnp.where(wide_lane == width - 1, right, pltpu.roll(lat, width - 1, 1))

    def row_of(r):
        return jnp.concatenate([blocks_ref[inv_ref[r * lanes + k]] for k in range(lanes)], axis=1)

    make_row(0, jnp.concatenate([rows_ref[0, k] for k in range(lanes)], axis=1))
    make_row(rows + 1, jnp.concatenate([rows_ref[1, k] for k in range(lanes)], axis=1))
    make_row(1, row_of(0))

    lane_w = lax.broadcasted_iota(jnp.int32, (8, width), 0)
    tail = (lane_w < chans - (CP - 8)).astype(f32)
    ones_rows = (lane_w == chans - (CP - 8)) | (lane_w == chans - (CP - 8) + 1)

    def col_sum(v):
        return jnp.sum(v, axis=0, keepdims=True)

    def front(r, u):
        total = jnp.zeros((8, width), f32)
        for c in range(0, CP, 8):
            acc = None
            for tap in range(9):
                term = wide(kern_ref[tap, c : c + 8, :]) * field[r + tap // 3, tap % 3, c : c + 8, :]
                acc = term if acc is None else acc + term
            depth_s[u, c : c + 8, :] = acc
            total = total + acc
        mean = col_sum(total) * (1.0 / chans)
        square = jnp.zeros((8, width), f32)
        for c in range(0, CP, 8):
            d = depth_s[u, c : c + 8, :] - mean
            if c == CP - 8:
                d = d * tail
            depth_s[u, c : c + 8, :] = d
            square = square + d * d
        inv_std = lax.rsqrt(col_sum(square) * (1.0 / chans) + NORM_EPS)
        for c in range(0, CP, 16):
            parts = []
            for e in (c, c + 8):
                s = depth_s[u, e : e + 8, :] * inv_std
                scaled_s[u, e : e + 8, :] = s
                n = s * wide(vec_ref[1, e : e + 8, :]) + wide(vec_ref[2, e : e + 8, :])
                if e == CP - 8:
                    n = jnp.where(ones_rows, 1.0, n)
                parts.append(n)
            norm_s[u, c : c + 16, :] = jnp.concatenate(parts, axis=0).astype(bf16)
        cot = jnp.concatenate([cot_s[k, pl.ds(r, CP, stride=rows), :] for k in range(lanes)], axis=1)
        cotb_s[u] = cot.astype(bf16)
        pre_s[u] = jnp.dot(w1t_ref[...], norm_s[u], preferred_element_type=f32)
        back_s[u] = jnp.dot(w2_ref[...], cotb_s[u], preferred_element_type=f32)
        return inv_std

    def middle(u):
        for h in range(0, HP, 16):
            x = pre_s[u, h : h + 16, :]
            q = x * x
            t = jnp.tanh(x * (GELU_K + (GELU_K * GELU_C) * q))
            s = 0.5 + 0.5 * t
            g = x * s
            slope = s + (g - g * s) * (2.0 * GELU_K + (6.0 * GELU_K * GELU_C) * q)
            hid_s[u, h : h + 16, :] = g.astype(bf16)
            bp_s[u, h : h + 16, :] = (back_s[u, h : h + 16, :] * slope).astype(bf16)

    def rear(r, u, inv_std):
        out = jnp.dot(w2t_ref[...], hid_s[u], preferred_element_type=f32)
        out = out + wide(vec_ref[3]) + field[r + 1, 1]
        for k in range(lanes):
            out_s[k, pl.ds(r, CP, stride=rows), :] = out[:, k * 128 : (k + 1) * 128]
        bd_s[u] = jnp.dot(w1_ref[...], bp_s[u], preferred_element_type=f32)
        one = jnp.zeros((8, width), f32)
        two = jnp.zeros((8, width), f32)
        for c in range(0, CP, 8):
            b = bd_s[u, c : c + 8, :] * wide(vec_ref[1, c : c + 8, :])
            bd_s[u, c : c + 8, :] = b
            one = one + b
            two = two + b * scaled_s[u, c : c + 8, :]
        one = col_sum(one) * (inv_std * (1.0 / chans))
        two = col_sum(two) * (inv_std * (1.0 / chans))
        for c in range(0, CP, 8):
            b = bd_s[u, c : c + 8, :] * inv_std - one - scaled_s[u, c : c + 8, :] * two
            for tap in range(9):
                m = b * field[r + tap // 3, tap % 3, c : c + 8, :]
                m = sum(m[:, k * 128 : (k + 1) * 128] for k in range(lanes))
                gk_s[tap, c : c + 8, :] += m

    def step(i, _):
        stds = []
        for u in range(UNROLL):
            r = i * UNROLL + u
            nxt = jnp.minimum(r + 1, rows - 1)
            make_row(nxt + 1, row_of(nxt))
        for u in range(UNROLL):
            stds.append(front(i * UNROLL + u, u))
        for u in range(UNROLL):
            middle(u)
        for u in range(UNROLL):
            rear(i * UNROLL + u, u, stds[u])
        nt = (((1,), (1,)), ((), ()))
        g2_s[...] += sum(lax.dot_general(hid_s[u], cotb_s[u], nt, preferred_element_type=f32) for u in range(UNROLL))
        g1_s[...] += sum(lax.dot_general(bp_s[u], norm_s[u], nt, preferred_element_type=f32) for u in range(UNROLL))
        return 0

    lax.fori_loop(0, rows // UNROLL, step, 0)

    def back(c, _):
        x = jnp.concatenate(
            [out_s[k, pl.ds(pl.multiple_of(c * rows, rows), rows), :] for k in range(lanes)], axis=1
        )
        out_ref[c] = x.astype(bf16)
        return 0

    lax.fori_loop(0, chans, back, 0)
    grad_ref[...] = jnp.zeros_like(grad_ref)
    grad_ref[0:360, 0:CP] = g2_s[0:360, :] * scale
    grad_ref[360:720, 0:CP] = g1_s[0:360, :] * scale
    ones = jnp.ones((8, 128), f32)
    for tap in range(9):
        line = lax.dot_general(
            ones, gk_s[tap], (((1,), (1,)), ((), ())), preferred_element_type=f32, precision=lax.Precision.HIGHEST
        )
        grad_ref[720 + tap : 721 + tap, 0:CP] = line[0:1, :] * scale


def strip_call(inv, flags, blocks, rows, cols, cot, w_in, b_in, kernel, ln_gain, ln_bias, w_one, b_one, w_two, b_two, scale):
    chans, nrow, width = cot.shape
    pad_c = CP - chans
    pad_h = HP - w_one.shape[1]
    win = jnp.pad(w_in.T, ((0, pad_c), (0, 0)))
    table = jnp.pad(jnp.concatenate([jnp.stack([b_in, ln_gain, ln_bias, b_two]), kernel]), ((0, 0), (0, pad_c)))
    table = jnp.broadcast_to(table[:, :, None], (13, CP, 128))
    vec, kern = table[:4], table[4:]
    high = b_one.astype(jnp.bfloat16)
    low = (b_one - high.astype(jnp.float32)).astype(jnp.bfloat16)
    w1t = jnp.pad(jnp.concatenate([w_one, high[None], low[None]]).T, ((0, pad_h), (0, pad_c - 2)))
    w2t = jnp.pad(w_two.T, ((0, pad_c), (0, pad_h)))
    w1 = jnp.pad(w_one, ((0, pad_c), (0, pad_h)))
    w2 = jnp.pad(w_two, ((0, pad_h), (0, pad_c)))
    f32, bf16 = jnp.float32, jnp.bfloat16
    lanes = width // 128
    vm = pl.BlockSpec(memory_space=pltpu.VMEM)
    sm = pl.BlockSpec(memory_space=pltpu.SMEM)
    return pl.pallas_call(
        functools.partial(strip_kernel, scale=scale),
        out_shape=(jax.ShapeDtypeStruct((chans, nrow, width), bf16), jax.ShapeDtypeStruct((768, 128), f32)),
        in_specs=[sm, sm] + [vm] * 11,
        out_specs=(vm, vm),
        scratch_shapes=[
            pltpu.VMEM((nrow + 2, 3, CP, width), f32),
            pltpu.VMEM((2, CP, 128), f32),
            pltpu.VMEM((lanes, CP * nrow, 128), f32),
            pltpu.VMEM((lanes, CP * nrow, 128), f32),
            pltpu.VMEM((UNROLL, CP, width), f32),
            pltpu.VMEM((UNROLL, CP, width), f32),
            pltpu.VMEM((UNROLL, CP, width), bf16),
            pltpu.VMEM((UNROLL, CP, width), bf16),
            pltpu.VMEM((UNROLL, HP, width), f32),
            pltpu.VMEM((UNROLL, HP, width), f32),
            pltpu.VMEM((UNROLL, HP, width), bf16),
            pltpu.VMEM((UNROLL, HP, width), bf16),
            pltpu.VMEM((UNROLL, CP, width), f32),
            pltpu.VMEM((HP, CP), f32),
            pltpu.VMEM((HP, CP), f32),
            pltpu.VMEM((9, CP, 128), f32),
        ],
        compiler_params=pltpu.CompilerParams(vmem_limit_bytes=58 * MIB),
    )(inv, flags, blocks, rows, cols, cot, win, vec, kern, w1t, w2t, w1, w2)


MESH = pl.DeviceIdType.MESH
MIB = 1024 * 1024
VM = pl.BlockSpec(memory_space=pltpu.VMEM)
SM = pl.BlockSpec(memory_space=pltpu.SMEM)
AXES = ("face", "tile")


def partial_kernel(pick_ref, slot_ref, source_ref, weight_ref, out_ref, part):
    count = weight_ref.shape[0]
    group = 8

    def one(i, _):
        for k in range(group):
            e = i * group + k
            x = jnp.dot(source_ref[pick_ref[e]], weight_ref[e], preferred_element_type=jnp.float32)
            part[e] = x.astype(jnp.bfloat16)
        return 0

    lax.fori_loop(0, count // group, one, 0)

    def put(d, _):
        out_ref[d, 0:16, :] = part[slot_ref[2 * d]]
        out_ref[d, 16:32, :] = part[slot_ref[2 * d + 1]]
        return 0

    lax.fori_loop(0, count, put, 0, unroll=8)


def partial_call(pick, slots, source, weight):
    count = weight.shape[0]
    return pl.pallas_call(
        partial_kernel,
        out_shape=jax.ShapeDtypeStruct((count, 32, 128), jnp.bfloat16),
        in_specs=[SM, SM, VM, VM],
        out_specs=VM,
        scratch_shapes=[pltpu.VMEM((count, 16, 128), jnp.bfloat16)],
        compiler_params=pltpu.CompilerParams(vmem_limit_bytes=32 * MIB),
    )(pick, slots, source, weight)


def exchange_kernel(faces, tiles, index, *refs):
    if index:
        ids_ref, box_ref, all_ref, got_ref, send, recv, local, send_a, recv_a, send_b, recv_b = refs
    else:
        box_ref, got_ref, send, recv, local = refs
    face = lax.axis_index("face")
    tile = lax.axis_index("tile")
    count = faces * tiles
    me = face * tiles + tile
    barrier = pltpu.get_barrier_semaphore()

    def greet(k, _):
        peer = lax.rem(me + k, count)
        pl.semaphore_signal(barrier, inc=1, device_id=(peer // tiles, lax.rem(peer, tiles)), device_id_type=MESH)
        return 0

    lax.fori_loop(1, count, greet, 0)
    pl.semaphore_wait(barrier, count - 1)

    if index:
        all_ref[face, tile] = ids_ref[...]
        first = []
        for k in range(1, tiles):
            first.append(
                pltpu.make_async_remote_copy(
                    src_ref=ids_ref,
                    dst_ref=all_ref.at[face, tile],
                    send_sem=send_a.at[k],
                    recv_sem=recv_a.at[k],
                    device_id=(face, lax.rem(tile + k, tiles)),
                    device_id_type=MESH,
                )
            )
            first[-1].start()

    def push(k, _):
        peer = lax.rem(me + k, count)
        pltpu.make_async_remote_copy(
            src_ref=box_ref.at[peer],
            dst_ref=got_ref.at[me],
            send_sem=send,
            recv_sem=recv,
            device_id=(peer // tiles, lax.rem(peer, tiles)),
            device_id_type=MESH,
        ).start()
        return 0

    lax.fori_loop(1, count, push, 0)
    own = pltpu.make_async_copy(box_ref.at[me], got_ref.at[me], local)
    own.start()
    if index:
        for copy in first:
            copy.wait()
        second = []
        for k in range(1, faces):
            second.append(
                pltpu.make_async_remote_copy(
                    src_ref=all_ref.at[face],
                    dst_ref=all_ref.at[face],
                    send_sem=send_b.at[k],
                    recv_sem=recv_b.at[k],
                    device_id=(lax.rem(face + k, faces), tile),
                    device_id_type=MESH,
                )
            )
            second[-1].start()
        for copy in second:
            copy.wait()
    own.wait()
    whole = pl.ds(0, count - 1)
    pltpu.make_async_copy(box_ref.at[whole], got_ref.at[whole], send).wait()
    pltpu.make_async_copy(box_ref.at[whole], got_ref.at[whole], recv).wait()


def exchange_call(box, ids, collective_id):
    faces, tiles = lax.axis_size("face"), lax.axis_size("tile")
    index = ids is not None
    out = [jax.ShapeDtypeStruct(box.shape, box.dtype)]
    args = [box]
    dma = pltpu.SemaphoreType.DMA
    scratch = [dma, dma, dma]
    if index:
        out = [jax.ShapeDtypeStruct((faces, tiles) + ids.shape, ids.dtype)] + out
        args = [ids] + args
        scratch += [dma((tiles,)), dma((tiles,)), dma((faces,)), dma((faces,))]
    return pl.pallas_call(
        functools.partial(exchange_kernel, faces, tiles, index),
        out_shape=tuple(out),
        in_specs=[VM] * len(args),
        out_specs=tuple([VM] * len(out)),
        scratch_shapes=scratch,
        compiler_params=pltpu.CompilerParams(
            collective_id=collective_id, has_side_effects=True, vmem_limit_bytes=32 * MIB
        ),
    )(*args)


def combine_kernel(label_ref, perm_ref, got_ref, out_ref, total):
    count = got_ref.shape[0]
    total[...] = jnp.zeros_like(total)

    def add(s, _):
        for k in range(2):
            spot = label_ref[2 * s + k]
            total[spot] += got_ref[s, 16 * k : 16 * k + 16, :].astype(jnp.float32)
        return 0

    lax.fori_loop(0, count, add, 0)

    def put(d, _):
        out_ref[d] = total[perm_ref[d]].astype(jnp.bfloat16)
        return 0

    lax.fori_loop(0, count, put, 0, unroll=8)


def combine_call(labels, perm, got):
    count = got.shape[0]
    return pl.pallas_call(
        combine_kernel,
        out_shape=jax.ShapeDtypeStruct((count, 16, 128), jnp.bfloat16),
        in_specs=[SM, SM, VM],
        out_specs=VM,
        scratch_shapes=[pltpu.VMEM((count + 1, 16, 128), jnp.float32)],
        compiler_params=pltpu.CompilerParams(vmem_limit_bytes=32 * MIB),
    )(labels, perm, got)


def lines_kernel(
    faces, tiles, inv_ref, link_ref, box_ref, rows_ref, cols_ref, edge, upper, lower, packet, packets, ends, line, wins,
    lots, windows, whole, send_v, recv_v, send_p, recv_p, send_e, recv_e, send_w, recv_w, send_l, recv_l,
):
    f32, bf16 = jnp.float32, jnp.bfloat16
    face = lax.axis_index("face")
    tile = lax.axis_index("tile")
    chans = box_ref.shape[1]
    nrow = box_ref.shape[0] // 4
    barrier = pltpu.get_barrier_semaphore()
    for k in range(1, tiles):
        pl.semaphore_signal(barrier, inc=1, device_id=(face, lax.rem(tile + k, tiles)), device_id_type=MESH)
    for k in range(1, faces):
        pl.semaphore_signal(barrier, inc=1, device_id=(lax.rem(face + k, faces), tile), device_id_type=MESH)
    pl.semaphore_wait(barrier, tiles + faces - 2)

    for k in range(4):
        edge[0, k] = box_ref[inv_ref[k]]
        edge[1, k] = box_ref[inv_ref[4 * nrow - 4 + k]]
    down = lax.rem(tile + 1, tiles)
    up = lax.rem(tile + tiles - 1, tiles)
    vertical = []
    for k, (dst, peer) in enumerate(((upper, down), (lower, up))):
        vertical.append(
            pltpu.make_async_remote_copy(
                src_ref=edge.at[1 - k],
                dst_ref=dst,
                send_sem=send_v.at[k],
                recv_sem=recv_v.at[k],
                device_id=(face, peer),
                device_id_type=MESH,
            )
        )
        vertical[-1].start()

    def end_copy(k, side):
        return pltpu.make_async_remote_copy(
            src_ref=edge.at[side],
            dst_ref=ends.at[side],
            send_sem=send_e.at[k],
            recv_sem=recv_e.at[side],
            device_id=(face, lax.rem(tile + k, tiles)),
            device_id_type=MESH,
        )

    for side, owner in ((0, 0), (1, tiles - 1)):

        @pl.when(tile == owner)
        def _():
            for k in range(1, tiles):
                end_copy(k, side).start()
            ends[side] = edge[side]

    lane = lax.broadcasted_iota(jnp.int32, (chans, 128), 1)

    def pick(r, acc):
        left = pltpu.roll(box_ref[inv_ref[4 * r]].astype(f32), r, 1)
        right = pltpu.roll(box_ref[inv_ref[4 * r + 3]].astype(f32), r + nrow + 1, 1)
        return jnp.where(lane == r, left, jnp.where(lane == r + nrow, right, acc))

    packet[...] = lax.fori_loop(0, nrow, pick, jnp.zeros((chans, 128), f32), unroll=8).astype(bf16)
    packets[tile] = packet[...]
    sends = []
    for k in range(1, tiles):
        sends.append(
            pltpu.make_async_remote_copy(
                src_ref=packet,
                dst_ref=packets.at[tile],
                send_sem=send_p.at[k],
                recv_sem=recv_p.at[k],
                device_id=(face, lax.rem(tile + k, tiles)),
                device_id_type=MESH,
            )
        )
        sends[-1].start()
    for copy in sends:
        copy.wait()
    for side, owner in ((0, 0), (1, tiles - 1)):

        @pl.when(tile == owner)
        def _():
            for k in range(1, tiles):
                end_copy(k, side).wait_send()

        @pl.when(tile != owner)
        def _():
            end_copy(1, side).wait_recv()

    per = 128 // nrow
    for side in range(2):
        line[side] = jnp.concatenate([ends[side, k] for k in range(4)], axis=1).astype(f32)
        parts = []
        for block in range(tiles // per):
            acc = jnp.zeros((chans, 128), f32)
            for i in range(per):
                seg = packets[block * per + i].astype(f32)
                seg = pltpu.roll(seg, (128 + (i - side) * nrow) % 128, 1) if i != side else seg
                acc = jnp.where((lane >= i * nrow) & (lane < (i + 1) * nrow), seg, acc)
            parts.append(acc)
        line[2 + side] = jnp.concatenate(parts, axis=1)
    width = tiles * nrow
    for s in range(4):
        full = line[s]
        for k in range(4):
            lots[s, k] = full[:, k * 128 : (k + 1) * 128].astype(bf16)
        near = pltpu.roll(full, lax.rem(width + 1 - tile * nrow, width), 1)[:, 0:128]
        far = pltpu.roll(full, lax.rem(width + 65 - (tiles - 1 - tile) * nrow, width), 1)[:, 0:128]
        wins[s] = jnp.where(lane < 64, near, far).astype(bf16)
    windows[face] = wins[...]
    sends = []
    for k in range(1, faces):
        sends.append(
            pltpu.make_async_remote_copy(
                src_ref=wins,
                dst_ref=windows.at[face],
                send_sem=send_w.at[k],
                recv_sem=recv_w.at[k],
                device_id=(lax.rem(face + k, faces), tile),
                device_id_type=MESH,
            )
        )
        sends[-1].start()

    def lot_copy(k):
        return pltpu.make_async_remote_copy(
            src_ref=lots,
            dst_ref=whole.at[face],
            send_sem=send_l.at[k],
            recv_sem=recv_l.at[k],
            device_id=(lax.rem(face + k, faces), tile),
            device_id_type=MESH,
        )

    at_end = (tile == 0) | (tile == tiles - 1)

    @pl.when(at_end)
    def _():
        for k in range(1, faces):
            lot_copy(k).start()
        whole[face] = lots[...]

    for copy in vertical:
        copy.wait()
    for copy in sends:
        copy.wait()
    row = lax.broadcasted_iota(jnp.int32, (128, 128), 0)
    col = lax.broadcasted_iota(jnp.int32, (128, 128), 1)
    at = 4 * (face * 3)
    for side in range(2):
        base = (face * 4 + 2 + side) * 3
        view = windows[link_ref[base], link_ref[base + 1]]
        spot = jnp.where(link_ref[base + 2] == 1, 65 + nrow - col, col)
        turn = (row == spot).astype(bf16)
        cols_ref[side] = jnp.dot(view, turn, preferred_element_type=f32).astype(bf16)
        rows_ref[side] = (upper, lower)[side][...]

    @pl.when(at_end)
    def _():
        for k in range(1, faces):
            lot_copy(k).wait()

    for side, owner in ((0, 0), (1, tiles - 1)):

        @pl.when(tile == owner)
        def _():
            base = (face * 4 + side) * 3
            flip = link_ref[base + 2] == 1
            turn = (row == jnp.where(flip, 127 - col, col)).astype(bf16)
            for k in range(4):
                view = whole[link_ref[base], link_ref[base + 1], jnp.where(flip, 3 - k, k)]
                rows_ref[side, k] = jnp.dot(view, turn, preferred_element_type=f32).astype(bf16)


def lines_call(inv, links, box, collective_id):
    faces, tiles = lax.axis_size("face"), lax.axis_size("tile")
    dma = pltpu.SemaphoreType.DMA
    bf16 = jnp.bfloat16
    chans = box.shape[1]
    block = (4, chans, 128)
    return pl.pallas_call(
        functools.partial(lines_kernel, faces, tiles),
        out_shape=(jax.ShapeDtypeStruct((2,) + block, bf16), jax.ShapeDtypeStruct((2, chans, 128), bf16)),
        in_specs=[SM, SM, VM],
        out_specs=(VM, VM),
        scratch_shapes=[
            pltpu.VMEM((2,) + block, bf16),
            pltpu.VMEM(block, bf16),
            pltpu.VMEM(block, bf16),
            pltpu.VMEM((chans, 128), bf16),
            pltpu.VMEM((tiles, chans, 128), bf16),
            pltpu.VMEM((2,) + block, bf16),
            pltpu.VMEM((4, chans, 512), jnp.float32),
            pltpu.VMEM(block, bf16),
            pltpu.VMEM((4,) + block, bf16),
            pltpu.VMEM((faces,) + block, bf16),
            pltpu.VMEM((faces, 4) + block, bf16),
            dma((2,)), dma((2,)), dma((tiles,)), dma((tiles,)), dma((tiles,)), dma((2,)), dma((faces,)), dma((faces,)),
            dma((faces,)), dma((faces,)),
        ],
        compiler_params=pltpu.CompilerParams(
            collective_id=collective_id, has_side_effects=True, vmem_limit_bytes=32 * MIB
        ),
    )(inv, links, box)


def reduce_kernel(
    faces, tiles, grad_ref, one_ref, two_ref, ker_ref, first, part, second, mine, full, send_a, recv_a, send_b, recv_b,
    send_c, recv_c,
):
    face = lax.axis_index("face")
    tile = lax.axis_index("tile")
    size = grad_ref.shape[0] // tiles
    barrier = pltpu.get_barrier_semaphore()
    for k in range(1, tiles):
        pl.semaphore_signal(barrier, inc=1, device_id=(face, lax.rem(tile + k, tiles)), device_id_type=MESH)
    for k in range(1, faces):
        pl.semaphore_signal(barrier, inc=1, device_id=(lax.rem(face + k, faces), tile), device_id_type=MESH)
    pl.semaphore_wait(barrier, tiles + faces - 2)

    def spot(t):
        return pl.ds(pl.multiple_of(t * size, 8), size)

    copies = []
    for k in range(1, tiles):
        peer = lax.rem(tile + k, tiles)
        copies.append(
            pltpu.make_async_remote_copy(
                src_ref=grad_ref.at[spot(peer)],
                dst_ref=first.at[k],
                send_sem=send_a.at[k],
                recv_sem=recv_a.at[k],
                device_id=(face, peer),
                device_id_type=MESH,
            )
        )
        copies[-1].start()
    total = grad_ref[spot(tile), :]
    for k in range(1, tiles):
        copies[k - 1].wait_recv()
        total = total + first[k]
    part[...] = total
    second[face] = total
    later = []
    for k in range(1, faces):
        later.append(
            pltpu.make_async_remote_copy(
                src_ref=part,
                dst_ref=second.at[face],
                send_sem=send_b.at[k],
                recv_sem=recv_b.at[k],
                device_id=(lax.rem(face + k, faces), tile),
                device_id_type=MESH,
            )
        )
        later[-1].start()
    for copy in later:
        copy.wait_recv()
    total = second[0]
    for k in range(1, faces):
        total = total + second[k]
    mine[...] = total
    full[spot(tile), :] = total
    last = []
    for k in range(1, tiles):
        last.append(
            pltpu.make_async_remote_copy(
                src_ref=mine,
                dst_ref=full.at[spot(tile)],
                send_sem=send_c.at[k],
                recv_sem=recv_c.at[k],
                device_id=(face, lax.rem(tile + k, tiles)),
                device_id_type=MESH,
            )
        )
        last[-1].start()
    for copy in last:
        copy.wait_recv()
    two_ref[...] = full[0:360, 0:90]
    one_ref[...] = full[360:720, 0:128].T[0:90, :]
    ker_ref[...] = full[720:729, 0:90]
    for copy in copies + later + last:
        copy.wait_send()


def reduce_call(grad, collective_id):
    faces, tiles = lax.axis_size("face"), lax.axis_size("tile")
    dma = pltpu.SemaphoreType.DMA
    f32 = jnp.float32
    size = grad.shape[0] // tiles
    return pl.pallas_call(
        functools.partial(reduce_kernel, faces, tiles),
        out_shape=(
            jax.ShapeDtypeStruct((90, 360), f32),
            jax.ShapeDtypeStruct((360, 90), f32),
            jax.ShapeDtypeStruct((9, 90), f32),
        ),
        in_specs=[VM],
        out_specs=(VM, VM, VM),
        scratch_shapes=[
            pltpu.VMEM((tiles, size, 128), f32),
            pltpu.VMEM((size, 128), f32),
            pltpu.VMEM((faces, size, 128), f32),
            pltpu.VMEM((size, 128), f32),
            pltpu.VMEM(grad.shape, f32),
            dma((tiles,)), dma((tiles,)), dma((faces,)), dma((faces,)), dma((tiles,)), dma((tiles,)),
        ],
        compiler_params=pltpu.CompilerParams(
            collective_id=collective_id, has_side_effects=True, vmem_limit_bytes=32 * MIB
        ),
    )(grad)


def remap(source, entry_block, entry_source, entry_weight, lat_to_nested):
    count = entry_block.shape[0]
    me = lax.axis_index("face") * lax.axis_size("tile") + lax.axis_index("tile")
    ids = jnp.arange(count, dtype=jnp.int32)
    owner = entry_block // count
    hit = owner[None, :] == ids[:, None]
    low = jnp.min(jnp.where(hit, ids[None, :], count - 1), axis=1)
    high = jnp.max(jnp.where(hit, ids[None, :], 0), axis=1)
    slots = jnp.stack([low, high], axis=1).reshape(-1)
    perm = jnp.sum(jnp.where((lat_to_nested // count)[None, :] == ids[:, None], ids[None, :], 0), axis=1)
    box = partial_call(entry_source, slots, source, entry_weight)
    table, got = exchange_call(box, jnp.stack([entry_block, lat_to_nested]), 1)
    table = table.reshape(count, 2, count)
    key = ids[None, :] * count + table[:, 0] % count
    hit = table[:, 0] // count == me
    low = jnp.min(jnp.where(hit, key, count * count), axis=1)
    high = jnp.max(jnp.where(hit, key, -1), axis=1)
    label_low = jnp.where(high >= 0, low % count, count)
    label_high = jnp.where(high > low, high % count, count)
    labels = jnp.stack([label_low, label_high], axis=1).reshape(-1)
    spots = jnp.sum(jnp.where(table[:, 1] // count == me, table[:, 1] % count, 0), axis=1)
    inv = jnp.sum(jnp.where(spots[None, :] == ids[:, None], ids[None, :], 0), axis=1)
    out = combine_call(labels, perm, got)
    return inv, exchange_call(out, None, 2)[0]

def per_device(
    source, entry_block, entry_source, entry_weight, lat_to_nested, face_links, w_in, b_in, kernel, ln_gain, ln_bias,
    w_one, b_one, w_two, b_two, cotangent,
):
    tile_at = lax.axis_index("tile")
    face_count, tile_count = lax.axis_size("face"), lax.axis_size("tile")
    width = cotangent.shape[3]
    inv, box = remap(source, entry_block, entry_source, entry_weight, lat_to_nested)
    rows, cols = lines_call(inv, face_links.reshape(-1), box, 3)
    flags = jnp.stack([tile_at == 0, tile_at == tile_count - 1]).astype(jnp.int32)
    scale = 1.0 / math.sqrt(face_count * width * width)
    output, grad = strip_call(
        inv, flags, box, rows, cols, cotangent[0], w_in, b_in, kernel, ln_gain, ln_bias, w_one, b_one, w_two, b_two,
        scale,
    )
    grad_one, grad_two, grad_kernel = reduce_call(grad, 4)
    return (output[None], grad_one, grad_two, grad_kernel)


def solution(mesh):
    split = P(("face", "tile"))
    strips = P("face", None, "tile", None)
    return jax.shard_map(
        per_device,
        mesh=mesh,
        in_specs=(split,) * 5 + (P(),) * 10 + (strips,),
        out_specs=(strips, P(), P(), P()),
        check_vma=False,
    )
```

time: 601 us -> 185 us (0.31); the launches traced: 592 us -> 184 us
  Pallas kernels: 0 us -> 158 us
  waiting for transfers between devices: 132 us -> 0 us
  local copies, waits for them, and re-layouts: 130 us -> 20.8 us
  other arithmetic: 107 us -> 4.12 us
  blocking collectives: 90.3 us -> 0 us
  matrix products: 76 us -> 0 us
  starting transfers between devices: 41.4 us -> 0 us
  between operations: 14.6 us -> 0.82 us
    pallas_call x0 -> x7, Pallas kernels: none -> 158 us  [the longest x1 66.4 us: strip_call(): pl.pallas_call(functools.partial(strip_kernel, scale=scale), out_shape=(j...]
    psum x1 -> x0, waiting for transfers between devices: 77.2 us -> none  [per_device(): lax.psum((grad_one, grad_two, grad_kernel), ('face', 'tile'))]
    dot_general x8 -> x0, matrix products: 76 us -> none  [the longest x1 20.6 us: strip_work(): back_hidden = jnp.dot(w_two, cot_flat, preferred_element_type=jnp.float32)]
    reduce_sum x5 -> x2, other arithmetic: 70.9 us -> 0.21 us  [the longest x1 0.1 us: remap(): jnp.sum(jnp.where((lat_to_nested // count)[None, :] == ids[:, None], ids[...]
    psum x1 -> x0, blocking collectives: 67 us -> none  [per_device(): lax.psum((grad_one, grad_two, grad_kernel), ('face', 'tile'))]
    scatter x5 -> x0, local copies, waits for them, and re-layouts: 47 us -> none  [the longest x1 13.3 us: per_device(): outbox = jnp.zeros((dev_count, CAP, in_count, block_len), jnp.bfloat16).a...]
    all_to_all x4 -> x0, starting transfers between devices: 35.6 us -> none  [the longest x1 11.5 us: per_device(): lax.all_to_all(labels, ('face', 'tile'), split_axis=0, concat_axis=0, til...]
    all_gather x2 -> x0, waiting for transfers between devices: 28.6 us -> none  [the longest x1 24 us: per_device(): lax.all_gather(own_lines.reshape(-1), 'face', axis=0, tiled=True)]
  transfers between devices with their start and end apart: 9 -> 0, of which waited for: 5 -> 0; matrix products, arithmetic and copies ran while one was open for 16% -> 0% of each run, Pallas kernels for 0% -> 0%
where the time goes in v1:
time: 185 us; the launch traced here: 184 us
  Pallas kernels  158 us (85%)
  local copies, waits for them, and re-layouts  20.8 us (11%)
  other arithmetic  4.12 us (2%)
    pallas_call x1, Pallas kernels, strip_call(): pl.pallas_call(functools.partial(strip_kernel, scale=scale), out_shape=(j...  66.4 us
    pallas_call x2, Pallas kernels, exchange_call(): pl.pallas_call(functools.partial(exchange_kernel, faces, tiles, index), o...  45.2 us
    pallas_call x1, Pallas kernels, reduce_call(): pl.pallas_call(functools.partial(reduce_kernel, faces, tiles), out_shape=...  26.9 us
    pallas_call x1, Pallas kernels, lines_call(): pl.pallas_call(functools.partial(lines_kernel, faces, tiles), out_shape=(...  14 us
    unnamed x23, local copies, waits for them, and re-layouts  11.7 us
    pallas_call x1, Pallas kernels, partial_call(): pl.pallas_call(partial_kernel, out_shape=jax.ShapeDtypeStruct((count, 32,...  3.87 us

profile of v1, /device:TPU:1, one launch (start us, length us, event | category | flops | bytes accessed | tf_op | source)
XLA Modules:
  0.0 184.2 jit_solution(12999368999786146395)
XLA Ops:
  0.6 0.7 add_convert_fusion.flag_ref
  2.9 0.7 pad_add_fusion.refs_0_
  3.6 0.8 subtract_convert_fusion
  4.3 1.5 concatenate.6
  5.8 0.8 copy.29
  6.7 0.8 copy.30
  8.4 1.5 pad.26.w2t_ref
  10.0 1.5 pad.27.w1_ref
  11.7 1.0 copy.31
  13.5 1.0 copy.34
  14.5 0.7 pad.28.w2_ref
  15.2 0.8 broadcast_in_dim.76.vec_ref
  16.0 0.9 broadcast_in_dim.77.kern_ref
  16.9 2.2 %copy-done.1 = bf16[128,128,128]{2,1,0:T(8,128)(2,1)S(1)} copy-done((bf16[128,128,128]{2,1,0:T(8,128)(2,1)S(1)}, bf16[128,128,128]{2,1,0:T(8,128)(2,1)}, u32[]{:S(2)}) %copy-start.1) | copy-done | bytes 4194328
  19.1 0.9 copy-done.3
  20.7 3.9 %shard_map.183.refs_1_ = bf16[128,32,128]{2,1,0:T(8,128)(2,1)S(1)} custom-call(s32[128]{0:T(128)S(1)} %copy-done.7, s32[256]{0:T(256)S(1)} %reshape.124.slot_ref, bf16[64,16,128]{2,1,0:T(8,128)(2,1)S(1)} %copy-done.3, bf16[128,128,128]{2,1,0:T(8,128)(2,1)S(1)} %copy-done.1), custom_call_target="tpu_custom_call" | custom-call | tf_op jit(solution)/shard_map/pallas_call | solution.py:263
  24.6 28.0 %shard_map.184 = (s32[8,16,2,128]{3,2,1,0:T(2,128)S(1)}, bf16[128,32,128]{2,1,0:T(8,128)(2,1)S(1)}) custom-call(s32[2,128]{1,0:T(2,128)S(1)} %pad_add_fusion.refs_0_, bf16[128,32,128]{2,1,0:T(8,128)(2,1)S(1)} %shard_map.183.refs_1_), custom_call_target="tpu_custom_call" | custom-call | tf_op jit(solution)/shard_map/pallas_call | solution.py:358
  53.3 2.1 %shard_map.185.refs_0_ = bf16[128,16,128]{2,1,0:T(8,128)(2,1)S(1)} custom-call(s32[256]{0:T(256)S(1)} %reshape.126.label_ref, s32[128]{0:T(128)S(1)} %select_reduce_fusion.perm_ref, bf16[128,32,128]{2,1,0:T(8,128)(2,1)S(1)} %get-tuple-element.14.got_ref), custom_call_target="tpu_custom_call" | custom-call | tf_op jit(solution)/shard_map/pallas_call | solution.py:391
  55.4 17.2 %shard_map.186.box_ref.blocks_ref = bf16[128,16,128]{2,1,0:T(8,128)(2,1)S(1)} custom-call(bf16[128,16,128]{2,1,0:T(8,128)(2,1)S(1)} %shard_map.185.refs_0_), custom_call_target="tpu_custom_call" | custom-call | tf_op jit(solution)/shard_map/pallas_call | solution.py:358
  72.7 14.0 %shard_map.187 = (bf16[2,4,16,128]{3,2,1,0:T(8,128)(2,1)S(1)}, bf16[2,16,128]{2,1,0:T(8,128)(2,1)S(1)}) custom-call(s32[128]{0:T(128)S(1)} %select_reduce_fusion.3.inv_ref, s32[96]{0:T(128)S(1)} %reshape.127.link_ref, bf16[128,16,128]{2,1,0:T(8,128)(2,1)S(1)} %shard_map.186.box_ref.blocks_ref), custom_call_target="tpu_custom_call" | custom-call | tf_op jit(solution)/shard_map/pallas_call | solution.py:580
  87.9 66.4 %shard_map.188 = (bf16[90,32,512]{2,1,0:T(8,128)(2,1)}, f32[768,128]{1,0:T(8,128)}) custom-call(s32[128]{0:T(128)} %copy-done.6, s32[2]{0:T(128)} %add_convert_fusion.flag_ref, bf16[128,16,128]{2,1,0:T(8,128)(2,1)} %copy-done, bf16[2,4,16,128]{3,2,1,0:T(8,128)(2,1)} %copy-done.4, bf16[2,16,128]{2,1,0:T(8,128)(2,1)} %copy-done.5, ...), custom_call_target="tpu_custom_call" | custom-call | tf_op jit(solution)/shard_map/pallas_call | solution.py:206
  154.3 1.0 copy-done.2
  155.3 26.9 %shard_map.189 = (f32[90,360]{1,0:T(8,128)S(1)}, f32[360,90]{1,0:T(8,128)S(1)}, f32[9,90]{1,0:T(8,128)S(1)}) custom-call(f32[768,128]{1,0:T(8,128)S(1)} %copy-done.2), custom_call_target="tpu_custom_call" | custom-call | tf_op jit(solution)/shard_map/pallas_call | solution.py:690
  182.2 0.8 copy.35
  (38 shorter events, 7.4 us)
Async XLA Ops:
  16.9 2.2 %copy-start.1 = (bf16[128,128,128]{2,1,0:T(8,128)(2,1)S(1)}, bf16[128,128,128]{2,1,0:T(8,128)(2,1)}, u32[]{:S(2)}) copy-start(bf16[128,128,128]{2,1,0:T(8,128)(2,1)} %weight_ref.1) | copy-start | bytes 12582916
  19.1 0.9 copy-start.3
  20.1 0.7 copy-start.7
  53.1 34.8 %copy-start.6 = (s32[128]{0:T(128)}, s32[128]{0:T(128)S(1)}, u32[]{:S(2)}) copy-start(s32[128]{0:T(128)S(1)} %select_reduce_fusion.3.inv_ref) | copy-start | bytes 1540
  72.6 15.2 %copy-start = (bf16[128,16,128]{2,1,0:T(8,128)(2,1)}, bf16[128,16,128]{2,1,0:T(8,128)(2,1)S(1)}, u32[]{:S(2)}) copy-start(bf16[128,16,128]{2,1,0:T(8,128)(2,1)S(1)} %shard_map.186.box_ref.blocks_ref) | copy-start | bytes 1572868
  86.7 0.6 copy-start.4
  87.3 0.6 copy-start.5
  154.3 1.0 copy-start.2

commit v2 on v1

--- a/solution.py
+++ b/solution.py
@@ -14,152 +14,176 @@
 NORM_EPS = 1e-06
 CP = 96
 HP = 368
+PITCH = 40
 UNROLL = 2
+HID = 16
 MIB = 1024 * 1024
 
 
 def strip_kernel(
-    inv_ref, flag_ref, blocks_ref, rows_ref, cols_ref, cot_ref, win_ref, vec_ref, kern_ref, w1t_ref, w2t_ref, w1_ref,
-    w2_ref, out_ref, grad_ref, field, cols, cot_s, out_s, depth_s, scaled_s, norm_s, cotb_s, pre_s, back_s, hid_s, bp_s,
-    bd_s, g2_s, g1_s, gk_s, scale,
+    inv_ref, flag_ref, blocks_ref, rows_ref, cols_ref, cot_ref, win_ref, bin_ref, ker_ref, gain_ref, bias_ref, wone_ref,
+    bone_ref, wtwo_ref, btwo_ref, out_ref, grad_ref, field, cols, depth, cot_s, out_s, scaled_s, norm_s, cotb_s,
+    pre_s, back_s, hid_s, bp_s, g2_s, g1_s, gk_s, tab_s, vec_s, flat_s, tall_s, w_in_s, w1t_s, w1_s, w2t_s, w2_s, scale,
 ):
     chans, rows, width = cot_ref.shape
+    hidden = wone_ref.shape[1]
     lanes = width // 128
-    f32 = jnp.float32
-    bf16 = jnp.bfloat16
+    f32, bf16 = jnp.float32, jnp.bfloat16
+    nt = (((1,), (1,)), ((), ()))
 
     def wide(v):
         return jnp.concatenate([v] * lanes, axis=1)
 
-    def lift(x):
-        return (jnp.dot(win_ref[...], x, preferred_element_type=f32)).astype(bf16)
-
-    b_in = vec_ref[0]
+    tab_s[...] = jnp.zeros_like(tab_s)
+    for j, ref in enumerate((bin_ref, gain_ref, bias_ref, btwo_ref)):
+        tab_s[j : j + 1, 0:chans] = ref[...]
+    tab_s[4:13, 0:chans] = ker_ref[...]
+    turned = tab_s[...].T
+    for j in range(13):
+        vec_s[j] = jnp.broadcast_to(turned[0:CP, j : j + 1], (CP, 128))
+    tab_s[...] = jnp.zeros_like(tab_s)
+    tab_s[0:16, 0:chans] = win_ref[...].astype(f32)
+    w_in_s[...] = tab_s[...].T[0:CP, 0:16].astype(bf16)
+    flat_s[...] = jnp.zeros_like(flat_s)
+    flat_s[0:chans, 0:hidden] = wone_ref[...].astype(f32)
+    w1_s[...] = flat_s[0:CP, 0:HP].astype(bf16)
+    high = bone_ref[...].astype(bf16).astype(f32)
+    flat_s[chans : chans + 1, 0:hidden] = high
+    flat_s[chans + 1 : chans + 2, 0:hidden] = bone_ref[...] - high
+    w1t_s[...] = (flat_s[...].T[0:HP, 0:CP] * 0.5).astype(bf16)
+    tall_s[...] = jnp.zeros_like(tall_s)
+    tall_s[0:hidden, 0:chans] = wtwo_ref[...].astype(f32)
+    w2_s[...] = (tall_s[0:HP, 0:CP] * 0.5).astype(bf16)
+    w2t_s[...] = tall_s[...].T[0:CP, 0:HP].astype(bf16)
+
     lane = lax.broadcasted_iota(jnp.int32, (CP, 128), 1)
     last = lane == jnp.where(flag_ref[1] == 1, rows + 1, -1)
     first = lane == jnp.where(flag_ref[0] == 1, 0, -1)
     for side in range(2):
-        v = jnp.dot(win_ref[...], cols_ref[side], preferred_element_type=f32) + b_in
-        v = v.astype(bf16).astype(f32)
-        cols[side] = jnp.where(first | last, 0.0, v)
+        v = jnp.dot(w_in_s[...], cols_ref[side], preferred_element_type=f32) + vec_s[0]
+        cols[side] = jnp.where(first | last, 0.0, v.astype(bf16).astype(f32))
 
     g2_s[...] = jnp.zeros_like(g2_s)
     g1_s[...] = jnp.zeros_like(g1_s)
-    gk_s[...] = jnp.zeros_like(gk_s)
-    cot_s[:, chans * rows :, :] = jnp.zeros((lanes, (CP - chans) * rows, 128), f32)
+    cot_s[:, chans * PITCH :, :] = jnp.zeros((lanes, (CP - chans) * PITCH, 128), f32)
 
     def turn(c, _):
         x = cot_ref[c].astype(f32)
         for k in range(lanes):
-            cot_s[k, pl.ds(pl.multiple_of(c * rows, rows), rows), :] = x[:, k * 128 : (k + 1) * 128]
-        return 0
-
-    lax.fori_loop(0, chans, turn, 0)
+            cot_s[k, pl.ds(pl.multiple_of(c * PITCH, 8), rows), :] = x[:, k * 128 : (k + 1) * 128]
+        return 0
+
+    lax.fori_loop(0, chans, turn, 0, unroll=2)
 
     def make_row(at, x):
-        lat = jnp.dot(win_ref[...], x, preferred_element_type=f32) + wide(b_in)
+        lat = jnp.dot(w_in_s[...], x, preferred_element_type=f32) + wide(vec_s[0])
         lat = lat.astype(bf16).astype(f32)
-        wide_lane = lax.broadcasted_iota(jnp.int32, (CP, width), 1)
-        left = wide(pltpu.roll(cols[0], lax.rem(128 - at, 128), 1))
-        right = wide(pltpu.roll(cols[1], 127 - at, 1))
-        field[at, 0] = jnp.where(wide_lane == 0, left, pltpu.roll(lat, 1, 1))
-        field[at, 1] = lat
-        field[at, 2] = jnp.where(wide_lane == width - 1, right, pltpu.roll(lat, width - 1, 1))
-
-    def row_of(r):
-        return jnp.concatenate([blocks_ref[inv_ref[r * lanes + k]] for k in range(lanes)], axis=1)
+        wide_lane = lax.broadcasted_iota(jnp.int32, (CP, 128), 1)
+        mid = [lat[:, k * 128 : (k + 1) * 128] for k in range(lanes)]
+        up = [pltpu.roll(cols[0], lax.rem(128 - at, 128), 1)] + [pltpu.roll(m, 1, 1) for m in mid]
+        dn = [pltpu.roll(m, 127, 1) for m in mid] + [pltpu.roll(cols[1], 127 - at, 1)]
+        for k in range(lanes):
+            part = slice(k * 128, (k + 1) * 128)
+            field[at, 0, :, part] = jnp.where(wide_lane == 0, up[k], up[k + 1])
+            field[at, 1, :, part] = mid[k]
+            field[at, 2, :, part] = jnp.where(wide_lane == 127, dn[k + 1], dn[k])
 
     make_row(0, jnp.concatenate([rows_ref[0, k] for k in range(lanes)], axis=1))
     make_row(rows + 1, jnp.concatenate([rows_ref[1, k] for k in range(lanes)], axis=1))
-    make_row(1, row_of(0))
-
-    lane_w = lax.broadcasted_iota(jnp.int32, (8, width), 0)
-    tail = (lane_w < chans - (CP - 8)).astype(f32)
-    ones_rows = (lane_w == chans - (CP - 8)) | (lane_w == chans - (CP - 8) + 1)
+
+    def row_step(r, _):
+        make_row(r + 1, jnp.concatenate([blocks_ref[inv_ref[r * lanes + k]] for k in range(lanes)], axis=1))
+        return 0
+
+    lax.fori_loop(0, rows, row_step, 0, unroll=2)
+
+    def shifted(r, c):
+        return [
+            [field[r, side, pl.ds(c, 8), k * 128 : (k + 1) * 128] for k in range(lanes)] for side in range(3)
+        ]
+
+    def conv_chunk(i, _):
+        c = pl.multiple_of(i * 8, 8)
+        w = [vec_s[4 + tap, pl.ds(c, 8), :] for tap in range(9)]
+
+        def mix(a, views, k):
+            return w[3 * a] * views[0][k] + w[3 * a + 1] * views[1][k] + w[3 * a + 2] * views[2][k]
+
+        v0, v1 = shifted(0, c), shifted(1, c)
+        one = tuple(mix(0, v0, k) + mix(1, v1, k) for k in range(lanes))
+        two = tuple(mix(0, v1, k) for k in range(lanes))
+
+        def go(r, carry):
+            one, two = carry
+            v = shifted(r + 2, c)
+            for k in range(lanes):
+                depth[r, pl.ds(c, 8), k * 128 : (k + 1) * 128] = one[k] + mix(2, v, k)
+            return (
+                tuple(two[k] + mix(1, v, k) for k in range(lanes)),
+                tuple(mix(0, v, k) for k in range(lanes)),
+            )
+
+        lax.fori_loop(0, rows, go, (one, two), unroll=4)
+        return 0
+
+    lax.fori_loop(0, CP // 8, conv_chunk, 0)
+
+    row_id = lax.broadcasted_iota(jnp.int32, (CP, 128), 0)
+    real = row_id < chans
+    ones_rows = (row_id == chans) | (row_id == chans + 1)
 
     def col_sum(v):
         return jnp.sum(v, axis=0, keepdims=True)
 
     def front(r, u):
-        total = jnp.zeros((8, width), f32)
-        for c in range(0, CP, 8):
-            acc = None
-            for tap in range(9):
-                term = wide(kern_ref[tap, c : c + 8, :]) * field[r + tap // 3, tap % 3, c : c + 8, :]
-                acc = term if acc is None else acc + term
-            depth_s[u, c : c + 8, :] = acc
-            total = total + acc
-        mean = col_sum(total) * (1.0 / chans)
-        square = jnp.zeros((8, width), f32)
-        for c in range(0, CP, 8):
-            d = depth_s[u, c : c + 8, :] - mean
-            if c == CP - 8:
-                d = d * tail
-            depth_s[u, c : c + 8, :] = d
-            square = square + d * d
-        inv_std = lax.rsqrt(col_sum(square) * (1.0 / chans) + NORM_EPS)
-        for c in range(0, CP, 16):
-            parts = []
-            for e in (c, c + 8):
-                s = depth_s[u, e : e + 8, :] * inv_std
-                scaled_s[u, e : e + 8, :] = s
-                n = s * wide(vec_ref[1, e : e + 8, :]) + wide(vec_ref[2, e : e + 8, :])
-                if e == CP - 8:
-                    n = jnp.where(ones_rows, 1.0, n)
-                parts.append(n)
-            norm_s[u, c : c + 16, :] = jnp.concatenate(parts, axis=0).astype(bf16)
-        cot = jnp.concatenate([cot_s[k, pl.ds(r, CP, stride=rows), :] for k in range(lanes)], axis=1)
-        cotb_s[u] = cot.astype(bf16)
-        pre_s[u] = jnp.dot(w1t_ref[...], norm_s[u], preferred_element_type=f32)
-        back_s[u] = jnp.dot(w2_ref[...], cotb_s[u], preferred_element_type=f32)
-        return inv_std
+        stds = []
+        for k in range(lanes):
+            part = slice(k * 128, (k + 1) * 128)
+            d = depth[r, :, part]
+            d = d - col_sum(d) * (1.0 / chans)
+            d = jnp.where(real, d, 0.0)
+            inv_std = lax.rsqrt(col_sum(d * d) * (1.0 / chans) + NORM_EPS)
+            s = d * inv_std
+            scaled_s[u, :, part] = s
+            n = jnp.where(ones_rows, 1.0, s * vec_s[1] + vec_s[2])
+            norm_s[u, :, part] = n.astype(bf16)
+            cotb_s[u, :, part] = cot_s[k, pl.ds(r, CP, stride=PITCH), :].astype(bf16)
+            stds.append(inv_std)
+        pre_s[u] = jnp.dot(w1t_s[...], norm_s[u], preferred_element_type=f32).astype(pre_s.dtype)
+        back_s[u] = jnp.dot(w2_s[...], cotb_s[u], preferred_element_type=f32).astype(back_s.dtype)
+        return stds
 
     def middle(u):
+        ty = pre_s.dtype
+        num = lambda v: jnp.asarray(v, ty)
         for h in range(0, HP, 16):
             x = pre_s[u, h : h + 16, :]
             q = x * x
-            t = jnp.tanh(x * (GELU_K + (GELU_K * GELU_C) * q))
-            s = 0.5 + 0.5 * t
-            g = x * s
-            slope = s + (g - g * s) * (2.0 * GELU_K + (6.0 * GELU_K * GELU_C) * q)
+            t = jnp.tanh(x * (num(2.0 * GELU_K) + num(8.0 * GELU_K * GELU_C) * q))
+            p = num(1.0) + t
+            g = x * p
+            slope = p + g * (num(1.0) - t) * (num(2.0 * GELU_K) + num(24.0 * GELU_K * GELU_C) * q)
             hid_s[u, h : h + 16, :] = g.astype(bf16)
             bp_s[u, h : h + 16, :] = (back_s[u, h : h + 16, :] * slope).astype(bf16)
 
-    def rear(r, u, inv_std):
-        out = jnp.dot(w2t_ref[...], hid_s[u], preferred_element_type=f32)
-        out = out + wide(vec_ref[3]) + field[r + 1, 1]
+    def rear(r, u, stds):
+        out = jnp.dot(w2t_s[...], hid_s[u], preferred_element_type=f32)
+        hat = jnp.dot(w1_s[...], bp_s[u], preferred_element_type=f32)
         for k in range(lanes):
-            out_s[k, pl.ds(r, CP, stride=rows), :] = out[:, k * 128 : (k + 1) * 128]
-        bd_s[u] = jnp.dot(w1_ref[...], bp_s[u], preferred_element_type=f32)
-        one = jnp.zeros((8, width), f32)
-        two = jnp.zeros((8, width), f32)
-        for c in range(0, CP, 8):
-            b = bd_s[u, c : c + 8, :] * wide(vec_ref[1, c : c + 8, :])
-            bd_s[u, c : c + 8, :] = b
-            one = one + b
-            two = two + b * scaled_s[u, c : c + 8, :]
-        one = col_sum(one) * (inv_std * (1.0 / chans))
-        two = col_sum(two) * (inv_std * (1.0 / chans))
-        for c in range(0, CP, 8):
-            b = bd_s[u, c : c + 8, :] * inv_std - one - scaled_s[u, c : c + 8, :] * two
-            for tap in range(9):
-                m = b * field[r + tap // 3, tap % 3, c : c + 8, :]
-                m = sum(m[:, k * 128 : (k + 1) * 128] for k in range(lanes))
-                gk_s[tap, c : c + 8, :] += m
+            part = slice(k * 128, (k + 1) * 128)
+            out_s[k, pl.ds(r, CP, stride=PITCH), :] = out[:, part] + vec_s[3] + field[r + 1, 1, :, part]
+            b = hat[:, part] * vec_s[1]
+            s = scaled_s[u, :, part]
+            one = col_sum(b) * (stds[k] * (1.0 / chans))
+            two = col_sum(b * s) * (stds[k] * (1.0 / chans))
+            depth[r, :, part] = b * stds[k] - one - s * two
 
     def step(i, _):
-        stds = []
-        for u in range(UNROLL):
-            r = i * UNROLL + u
-            nxt = jnp.minimum(r + 1, rows - 1)
-            make_row(nxt + 1, row_of(nxt))
-        for u in range(UNROLL):
-            stds.append(front(i * UNROLL + u, u))
+        stds = [front(i * UNROLL + u, u) for u in range(UNROLL)]
         for u in range(UNROLL):
             middle(u)
         for u in range(UNROLL):
             rear(i * UNROLL + u, u, stds[u])
-        nt = (((1,), (1,)), ((), ()))
         g2_s[...] += sum(lax.dot_general(hid_s[u], cotb_s[u], nt, preferred_element_type=f32) for u in range(UNROLL))
         g1_s[...] += sum(lax.dot_general(bp_s[u], norm_s[u], nt, preferred_element_type=f32) for u in range(UNROLL))
         return 0
@@ -167,67 +191,103 @@
     lax.fori_loop(0, rows // UNROLL, step, 0)
 
     def back(c, _):
-        x = jnp.concatenate(
-            [out_s[k, pl.ds(pl.multiple_of(c * rows, rows), rows), :] for k in range(lanes)], axis=1
-        )
+        x = jnp.concatenate([out_s[k, pl.ds(pl.multiple_of(c * PITCH, 8), rows), :] for k in range(lanes)], axis=1)
         out_ref[c] = x.astype(bf16)
         return 0
 
-    lax.fori_loop(0, chans, back, 0)
-    grad_ref[...] = jnp.zeros_like(grad_ref)
-    grad_ref[0:360, 0:CP] = g2_s[0:360, :] * scale
-    grad_ref[360:720, 0:CP] = g1_s[0:360, :] * scale
+    lax.fori_loop(0, chans, back, 0, unroll=2)
+
+    def kernel_chunk(i, _):
+        c = pl.multiple_of(i * 8, 8)
+
+        def grad_row(r):
+            return tuple(depth[r, pl.ds(c, 8), k * 128 : (k + 1) * 128] for k in range(lanes))
+
+        def fold(acc, a, b, views):
+            new = list(acc)
+            for s in range(3):
+                m = b[0] * views[s][0]
+                for k in range(1, lanes):
+                    m = m + b[k] * views[s][k]
+                new[3 * a + s] = new[3 * a + s] + m
+            return tuple(new)
+
+        acc = tuple(jnp.zeros((8, 128), f32) for _ in range(9))
+        b0 = grad_row(0)
+        acc = fold(acc, 0, b0, shifted(0, c))
+        b1 = grad_row(1)
+        v = shifted(1, c)
+        acc = fold(fold(acc, 0, b1, v), 1, b0, v)
+
+        def go(r, carry):
+            acc, b1, b0 = carry
+            v = shifted(r, c)
+            b = grad_row(r)
+            acc = fold(fold(fold(acc, 0, b, v), 1, b1, v), 2, b0, v)
+            return acc, b, b1
+
+        acc, b1, b0 = lax.fori_loop(2, rows, go, (acc, b1, b0), unroll=3)
+        v = shifted(rows, c)
+        acc = fold(fold(acc, 1, b1, v), 2, b0, v)
+        acc = fold(acc, 2, b1, shifted(rows + 1, c))
+        for tap in range(9):
+            gk_s[tap, pl.ds(c, 8), :] = acc[tap]
+        return 0
+
+    lax.fori_loop(0, CP // 8, kernel_chunk, 0)
+    grad_ref[720:768, :] = jnp.zeros((48, 128), f32)
+    grad_ref[0:hidden, 0:CP] = g2_s[0:hidden, :] * scale
+    grad_ref[hidden : 2 * hidden, 0:CP] = g1_s[0:hidden, :] * scale
     ones = jnp.ones((8, 128), f32)
     for tap in range(9):
-        line = lax.dot_general(
-            ones, gk_s[tap], (((1,), (1,)), ((), ())), preferred_element_type=f32, precision=lax.Precision.HIGHEST
-        )
+        line = lax.dot_general(ones, gk_s[tap], nt, preferred_element_type=f32, precision=lax.Precision.HIGHEST)
         grad_ref[720 + tap : 721 + tap, 0:CP] = line[0:1, :] * scale
 
 
 def strip_call(inv, flags, blocks, rows, cols, cot, w_in, b_in, kernel, ln_gain, ln_bias, w_one, b_one, w_two, b_two, scale):
     chans, nrow, width = cot.shape
-    pad_c = CP - chans
-    pad_h = HP - w_one.shape[1]
-    win = jnp.pad(w_in.T, ((0, pad_c), (0, 0)))
-    table = jnp.pad(jnp.concatenate([jnp.stack([b_in, ln_gain, ln_bias, b_two]), kernel]), ((0, 0), (0, pad_c)))
-    table = jnp.broadcast_to(table[:, :, None], (13, CP, 128))
-    vec, kern = table[:4], table[4:]
-    high = b_one.astype(jnp.bfloat16)
-    low = (b_one - high.astype(jnp.float32)).astype(jnp.bfloat16)
-    w1t = jnp.pad(jnp.concatenate([w_one, high[None], low[None]]).T, ((0, pad_h), (0, pad_c - 2)))
-    w2t = jnp.pad(w_two.T, ((0, pad_c), (0, pad_h)))
-    w1 = jnp.pad(w_one, ((0, pad_c), (0, pad_h)))
-    w2 = jnp.pad(w_two, ((0, pad_h), (0, pad_c)))
     f32, bf16 = jnp.float32, jnp.bfloat16
     lanes = width // 128
+    act = bf16 if HID == 16 else f32
     vm = pl.BlockSpec(memory_space=pltpu.VMEM)
     sm = pl.BlockSpec(memory_space=pltpu.SMEM)
+    mem = pltpu.VMEM
     return pl.pallas_call(
         functools.partial(strip_kernel, scale=scale),
         out_shape=(jax.ShapeDtypeStruct((chans, nrow, width), bf16), jax.ShapeDtypeStruct((768, 128), f32)),
-        in_specs=[sm, sm] + [vm] * 11,
+        in_specs=[sm, sm] + [vm] * 13,
         out_specs=(vm, vm),
         scratch_shapes=[
-            pltpu.VMEM((nrow + 2, 3, CP, width), f32),
-            pltpu.VMEM((2, CP, 128), f32),
-            pltpu.VMEM((lanes, CP * nrow, 128), f32),
-            pltpu.VMEM((lanes, CP * nrow, 128), f32),
-            pltpu.VMEM((UNROLL, CP, width), f32),
-            pltpu.VMEM((UNROLL, CP, width), f32),
-            pltpu.VMEM((UNROLL, CP, width), bf16),
-            pltpu.VMEM((UNROLL, CP, width), bf16),
-            pltpu.VMEM((UNROLL, HP, width), f32),
-            pltpu.VMEM((UNROLL, HP, width), f32),
-            pltpu.VMEM((UNROLL, HP, width), bf16),
-            pltpu.VMEM((UNROLL, HP, width), bf16),
-            pltpu.VMEM((UNROLL, CP, width), f32),
-            pltpu.VMEM((HP, CP), f32),
-            pltpu.VMEM((HP, CP), f32),
-            pltpu.VMEM((9, CP, 128), f32),
+            mem((nrow + 2, 3, CP, width), f32),
+            mem((2, CP, 128), f32),
+            mem((nrow, CP, width), f32),
+            mem((lanes, CP * PITCH, 128), f32),
+            mem((lanes, CP * PITCH, 128), f32),
+            mem((UNROLL, CP, width), f32),
+            mem((UNROLL, CP, width), bf16),
+            mem((UNROLL, CP, width), bf16),
+            mem((UNROLL, HP, width), act),
+            mem((UNROLL, HP, width), act),
+            mem((UNROLL, HP, width), bf16),
+            mem((UNROLL, HP, width), bf16),
+            mem((HP, CP), f32),
+            mem((HP, CP), f32),
+            mem((9, CP, 128), f32),
+            mem((16, 128), f32),
+            mem((13, CP, 128), f32),
+            mem((128, 384), f32),
+            mem((384, 128), f32),
+            mem((CP, 16), bf16),
+            mem((HP, CP), bf16),
+            mem((CP, HP), bf16),
+            mem((CP, HP), bf16),
+            mem((HP, CP), bf16),
         ],
         compiler_params=pltpu.CompilerParams(vmem_limit_bytes=58 * MIB),
-    )(inv, flags, blocks, rows, cols, cot, win, vec, kern, w1t, w2t, w1, w2)
+    )(
+        inv, flags, blocks, rows, cols, cot, w_in, b_in[None], kernel, ln_gain[None], ln_bias[None], w_one, b_one[None],
+        w_two, b_two[None],
+    )
 
 
 MESH = pl.DeviceIdType.MESH

time: 185 us -> 156 us (0.84)
  Pallas kernels: 158 us -> 139 us
  local copies, waits for them, and re-layouts: 20.8 us -> 12.4 us
    pallas_call x1, Pallas kernels: 66.4 us -> 46.8 us  [strip_call(): pl.pallas_call(functools.partial(strip_kernel, scale=scale), out_shape=(j...]
    pad x5 -> x0, local copies, waits for them, and re-layouts: 5 us -> none  [the longest x1 1.52 us: strip_call(): w1 = jnp.pad(w_one, ((0, pad_c), (0, pad_h)))]
    unnamed x23 -> x21, local copies, waits for them, and re-layouts: 11.7 us -> 10.5 us
where the time goes in v2:
time: 156 us; the launch traced here: 155 us
  Pallas kernels  139 us (89%)
  local copies, waits for them, and re-layouts  12.4 us (8%)
  other arithmetic  3.22 us (2%)
    pallas_call x1, Pallas kernels, strip_call(): pl.pallas_call(functools.partial(strip_kernel, scale=scale), out_shape=(j...  46.8 us
    pallas_call x2, Pallas kernels, exchange_call(): pl.pallas_call(functools.partial(exchange_kernel, faces, tiles, index), o...  45.2 us
    pallas_call x1, Pallas kernels, reduce_call(): pl.pallas_call(functools.partial(reduce_kernel, faces, tiles), out_shape=...  26.9 us
    pallas_call x1, Pallas kernels, lines_call(): pl.pallas_call(functools.partial(lines_kernel, faces, tiles), out_shape=(...  14 us
    unnamed x21, local copies, waits for them, and re-layouts  10.5 us
    pallas_call x1, Pallas kernels, partial_call(): pl.pallas_call(partial_kernel, out_shape=jax.ShapeDtypeStruct((count, 32,...  3.87 us

profile of v2, /device:TPU:1, one launch (start us, length us, event | category | flops | bytes accessed | tf_op | source)
XLA Modules:
  0.0 155.3 jit_solution(8348942008678179740)
XLA Ops:
  0.6 0.6 add_convert_fusion.flag_ref
  1.3 0.7 and_select_fusion.3
  2.0 0.7 and_select_fusion
  2.9 0.7 pad_add_fusion.refs_0_
  3.5 1.2 broadcast_in_dim.80.bone_ref
  4.8 0.8 copy.27
  5.9 1.6 %copy.28.wtwo_ref = bf16[360,90]{1,0:T(8,128)(2,1)} copy(bf16[360,90]{0,1:T(8,128)(2,1)} %param.29) | data formatting | bytes 129600 | tf_op args[13]
  7.6 2.2 %copy-done.1 = bf16[128,128,128]{2,1,0:T(8,128)(2,1)S(1)} copy-done((bf16[128,128,128]{2,1,0:T(8,128)(2,1)S(1)}, bf16[128,128,128]{2,1,0:T(8,128)(2,1)}, u32[]{:S(2)}) %copy-start.1) | copy-done | bytes 4194328
  9.8 0.9 copy-done.3
  10.7 0.7 copy-done.7
  11.4 3.9 %shard_map.183.refs_1_ = bf16[128,32,128]{2,1,0:T(8,128)(2,1)S(1)} custom-call(s32[128]{0:T(128)S(1)} %copy-done.7, s32[256]{0:T(256)S(1)} %reshape.122.slot_ref, bf16[64,16,128]{2,1,0:T(8,128)(2,1)S(1)} %copy-done.3, bf16[128,128,128]{2,1,0:T(8,128)(2,1)S(1)} %copy-done.1), custom_call_target="tpu_custom_call" | custom-call | tf_op jit(solution)/shard_map/pallas_call | solution.py:323
  15.2 28.0 %shard_map.184 = (s32[8,16,2,128]{3,2,1,0:T(2,128)S(1)}, bf16[128,32,128]{2,1,0:T(8,128)(2,1)S(1)}) custom-call(s32[2,128]{1,0:T(2,128)S(1)} %pad_add_fusion.refs_0_, bf16[128,32,128]{2,1,0:T(8,128)(2,1)S(1)} %shard_map.183.refs_1_), custom_call_target="tpu_custom_call" | custom-call | tf_op jit(solution)/shard_map/pallas_call | solution.py:418
  43.3 0.2 select_reduce_fusion.2
  43.9 2.1 %shard_map.185.refs_0_ = bf16[128,16,128]{2,1,0:T(8,128)(2,1)S(1)} custom-call(s32[256]{0:T(256)S(1)} %reshape.124.label_ref, s32[128]{0:T(128)S(1)} %select_reduce_fusion.perm_ref, bf16[128,32,128]{2,1,0:T(8,128)(2,1)S(1)} %get-tuple-element.14.got_ref), custom_call_target="tpu_custom_call" | custom-call | tf_op jit(solution)/shard_map/pallas_call | solution.py:451
  46.1 17.2 %shard_map.186.box_ref.blocks_ref = bf16[128,16,128]{2,1,0:T(8,128)(2,1)S(1)} custom-call(bf16[128,16,128]{2,1,0:T(8,128)(2,1)S(1)} %shard_map.185.refs_0_), custom_call_target="tpu_custom_call" | custom-call | tf_op jit(solution)/shard_map/pallas_call | solution.py:418
  63.3 14.0 %shard_map.187 = (bf16[2,4,16,128]{3,2,1,0:T(8,128)(2,1)S(1)}, bf16[2,16,128]{2,1,0:T(8,128)(2,1)S(1)}) custom-call(s32[128]{0:T(128)S(1)} %select_reduce_fusion.3.inv_ref, s32[96]{0:T(128)S(1)} %reshape.125.link_ref, bf16[128,16,128]{2,1,0:T(8,128)(2,1)S(1)} %shard_map.186.box_ref.blocks_ref), custom_call_target="tpu_custom_call" | custom-call | tf_op jit(solution)/shard_map/pallas_call | solution.py:640
  77.3 0.6 copy-done.4
  77.9 0.6 copy-done.5
  78.5 46.8 %shard_map.188 = (bf16[90,32,512]{2,1,0:T(8,128)(2,1)}, f32[768,128]{1,0:T(8,128)}) custom-call(s32[128]{0:T(128)} %copy-done.6, s32[2]{0:T(128)} %add_convert_fusion.flag_ref, bf16[128,16,128]{2,1,0:T(8,128)(2,1)} %copy-done, bf16[2,4,16,128]{3,2,1,0:T(8,128)(2,1)} %copy-done.4, bf16[2,16,128]{2,1,0:T(8,128)(2,1)} %copy-done.5, ...), custom_call_target="tpu_custom_call" | custom-call | tf_op jit(solution)/shard_map/pallas_call | solution.py:255
  125.3 1.0 copy-done.2
  126.3 26.9 %shard_map.189 = (f32[90,360]{1,0:T(8,128)S(1)}, f32[360,90]{1,0:T(8,128)S(1)}, f32[9,90]{1,0:T(8,128)S(1)}) custom-call(f32[768,128]{1,0:T(8,128)S(1)} %copy-done.2), custom_call_target="tpu_custom_call" | custom-call | tf_op jit(solution)/shard_map/pallas_call | solution.py:750
  153.2 0.8 copy.29
  154.0 0.7 copy.33
  154.7 0.6 copy.34
  (23 shorter events, 1.1 us)
Async XLA Ops:
  7.6 2.2 %copy-start.1 = (bf16[128,128,128]{2,1,0:T(8,128)(2,1)S(1)}, bf16[128,128,128]{2,1,0:T(8,128)(2,1)}, u32[]{:S(2)}) copy-start(bf16[128,128,128]{2,1,0:T(8,128)(2,1)} %weight_ref.1) | copy-start | bytes 12582916
  9.8 0.9 copy-start.3
  10.7 0.7 copy-start.7
  43.7 34.9 %copy-start.6 = (s32[128]{0:T(128)}, s32[128]{0:T(128)S(1)}, u32[]{:S(2)}) copy-start(s32[128]{0:T(128)S(1)} %select_reduce_fusion.3.inv_ref) | copy-start | bytes 1540
  63.3 15.2 %copy-start = (bf16[128,16,128]{2,1,0:T(8,128)(2,1)}, bf16[128,16,128]{2,1,0:T(8,128)(2,1)S(1)}, u32[]{:S(2)}) copy-start(bf16[128,16,128]{2,1,0:T(8,128)(2,1)S(1)} %shard_map.186.box_ref.blocks_ref) | copy-start | bytes 1572868
  77.3 0.6 copy-start.4
  77.9 0.6 copy-start.5
  125.3 1.0 copy-start.2

commit v3 on v2

v3 whole, which is shorter than its diff:
```python
import functools
import math

import jax
import jax.numpy as jnp
from jax import lax
from jax.experimental import pallas as pl
from jax.experimental.pallas import tpu as pltpu
from jax.sharding import PartitionSpec as P


GELU_K = 0.7978845608028654
GELU_C = 0.044715
NORM_EPS = 1e-06
CP = 96
HP = 368
PITCH = 40
UNROLL = 2
HID = 16
MIB = 1024 * 1024


def strip_kernel(
    blocks_ref, rows_ref, cols_ref, cot_ref, win_ref, bin_ref, ker_ref, gain_ref, bias_ref, wone_ref,
    bone_ref, wtwo_ref, btwo_ref, out_ref, grad_ref, field, cols, depth, cot_s, out_s, scaled_s, norm_s, cotb_s,
    pre_s, back_s, hid_s, bp_s, g2_s, g1_s, gk_s, tab_s, vec_s, flat_s, w_in_s, w1t_s, w1_s, w2t_s, w2_s, scale,
):
    chans, rows, width = cot_ref.shape
    hidden = wone_ref.shape[1]
    lanes = width // 128
    f32, bf16 = jnp.float32, jnp.bfloat16
    nt = (((1,), (1,)), ((), ()))

    def wide(v):
        return jnp.concatenate([v] * lanes, axis=1)

    tab_s[...] = jnp.zeros_like(tab_s)
    for j, ref in enumerate((bin_ref, gain_ref, bias_ref, btwo_ref)):
        tab_s[j : j + 1, 0:chans] = ref[...]
    tab_s[4:13, 0:chans] = ker_ref[...]
    turned = tab_s[...].T
    for j in range(13):
        vec_s[j] = jnp.broadcast_to(turned[0:CP, j : j + 1], (CP, 128))
    tab_s[...] = jnp.zeros_like(tab_s)
    tab_s[0:16, 0:chans] = win_ref[...].astype(f32)
    w_in_s[...] = tab_s[...].T[0:CP, 0:16].astype(bf16)
    flat_s[...] = jnp.zeros_like(flat_s)
    flat_s[0:chans, 0:hidden] = wone_ref[...].astype(f32)
    w1_s[...] = flat_s[0:CP, 0:HP].astype(bf16)
    high = bone_ref[...].astype(bf16).astype(f32)
    flat_s[chans : chans + 1, 0:hidden] = high
    flat_s[chans + 1 : chans + 2, 0:hidden] = bone_ref[...] - high
    w1t_s[...] = (flat_s[...].T[0:HP, 0:CP] * 0.5).astype(bf16)
    flat_s[...] = jnp.zeros_like(flat_s)
    flat_s[0:chans, 0:hidden] = wtwo_ref[...].astype(f32)
    w2t_s[...] = flat_s[0:CP, 0:HP].astype(bf16)
    w2_s[...] = (flat_s[...].T[0:HP, 0:CP] * 0.5).astype(bf16)

    tile, tile_count = lax.axis_index("tile"), lax.axis_size("tile")
    lane = lax.broadcasted_iota(jnp.int32, (CP, 128), 1)
    last = lane == jnp.where(tile == tile_count - 1, rows + 1, -1)
    first = lane == jnp.where(tile == 0, 0, -1)
    for side in range(2):
        v = jnp.dot(w_in_s[...], cols_ref[side], preferred_element_type=f32) + vec_s[0]
        cols[side] = jnp.where(first | last, 0.0, v.astype(bf16).astype(f32))

    g2_s[...] = jnp.zeros_like(g2_s)
    g1_s[...] = jnp.zeros_like(g1_s)
    cot_s[:, chans * PITCH :, :] = jnp.zeros((lanes, (CP + 1 - chans) * PITCH, 128), f32)

    def turn(c, _):
        x = cot_ref[c].astype(f32)
        for k in range(lanes):
            cot_s[k, pl.ds(pl.multiple_of(c * PITCH, 8), rows), :] = x[:, k * 128 : (k + 1) * 128]
        return 0

    lax.fori_loop(0, chans, turn, 0, unroll=2)

    def make_row(at, x):
        lat = jnp.dot(w_in_s[...], x, preferred_element_type=f32) + wide(vec_s[0])
        lat = lat.astype(bf16).astype(f32)
        wide_lane = lax.broadcasted_iota(jnp.int32, (CP, 128), 1)
        mid = [lat[:, k * 128 : (k + 1) * 128] for k in range(lanes)]
        up = [pltpu.roll(cols[0], lax.rem(128 - at, 128), 1)] + [pltpu.roll(m, 1, 1) for m in mid]
        dn = [pltpu.roll(m, 127, 1) for m in mid] + [pltpu.roll(cols[1], 127 - at, 1)]
        for k in range(lanes):
            part = slice(k * 128, (k + 1) * 128)
            field[at, 0, :, part] = jnp.where(wide_lane == 0, up[k], up[k + 1])
            field[at, 1, :, part] = mid[k]
            field[at, 2, :, part] = jnp.where(wide_lane == 127, dn[k + 1], dn[k])

    make_row(0, jnp.concatenate([rows_ref[0, k] for k in range(lanes)], axis=1))
    make_row(rows + 1, jnp.concatenate([rows_ref[1, k] for k in range(lanes)], axis=1))

    def row_step(r, _):
        make_row(r + 1, jnp.concatenate([blocks_ref[r * lanes + k] for k in range(lanes)], axis=1))
        return 0

    lax.fori_loop(0, rows, row_step, 0, unroll=2)

    def shifted(r, c):
        return [
            [field[r, side, pl.ds(c, 8), k * 128 : (k + 1) * 128] for k in range(lanes)] for side in range(3)
        ]

    def conv_chunk(i, _):
        c = pl.multiple_of(i * 8, 8)
        w = [vec_s[4 + tap, pl.ds(c, 8), :] for tap in range(9)]

        def mix(a, views, k):
            return w[3 * a] * views[0][k] + w[3 * a + 1] * views[1][k] + w[3 * a + 2] * views[2][k]

        v0, v1 = shifted(0, c), shifted(1, c)
        one = tuple(mix(0, v0, k) + mix(1, v1, k) for k in range(lanes))
        two = tuple(mix(0, v1, k) for k in range(lanes))

        def go(r, carry):
            one, two = carry
            v = shifted(r + 2, c)
            for k in range(lanes):
                depth[r, pl.ds(c, 8), k * 128 : (k + 1) * 128] = one[k] + mix(2, v, k)
            return (
                tuple(two[k] + mix(1, v, k) for k in range(lanes)),
                tuple(mix(0, v, k) for k in range(lanes)),
            )

        lax.fori_loop(0, rows, go, (one, two), unroll=4)
        return 0

    lax.fori_loop(0, CP // 8, conv_chunk, 0)

    row_id = lax.broadcasted_iota(jnp.int32, (CP, 128), 0)
    real = row_id < chans
    ones_rows = (row_id == chans) | (row_id == chans + 1)

    def col_sum(v):
        return jnp.sum(v, axis=0, keepdims=True)

    def front(r, u):
        stds = []
        for k in range(lanes):
            part = slice(k * 128, (k + 1) * 128)
            d = depth[r, :, part]
            d = d - col_sum(d) * (1.0 / chans)
            d = jnp.where(real, d, 0.0)
            inv_std = lax.rsqrt(col_sum(d * d) * (1.0 / chans) + NORM_EPS)
            s = d * inv_std
            scaled_s[u, :, part] = s
            n = jnp.where(ones_rows, 1.0, s * vec_s[1] + vec_s[2])
            norm_s[u, :, part] = n.astype(bf16)
            cotb_s[u, :, part] = cot_s[k, pl.ds(r, CP, stride=PITCH), :].astype(bf16)
            stds.append(inv_std)
        pre_s[u] = jnp.dot(w1t_s[...], norm_s[u], preferred_element_type=f32).astype(pre_s.dtype)
        back_s[u] = jnp.dot(w2_s[...], cotb_s[u], preferred_element_type=f32).astype(back_s.dtype)
        return stds

    def middle(u):
        ty = pre_s.dtype
        num = lambda v: jnp.asarray(v, ty)
        for h in range(0, HP, 16):
            x = pre_s[u, h : h + 16, :]
            q = x * x
            t = jnp.tanh(x * (num(2.0 * GELU_K) + num(8.0 * GELU_K * GELU_C) * q))
            p = num(1.0) + t
            g = x * p
            slope = p + g * (num(1.0) - t) * (num(2.0 * GELU_K) + num(24.0 * GELU_K * GELU_C) * q)
            hid_s[u, h : h + 16, :] = g.astype(bf16)
            bp_s[u, h : h + 16, :] = (back_s[u, h : h + 16, :] * slope).astype(bf16)

    def rear(r, u, stds):
        out = jnp.dot(w2t_s[...], hid_s[u], preferred_element_type=f32)
        hat = jnp.dot(w1_s[...], bp_s[u], preferred_element_type=f32)
        for k in range(lanes):
            part = slice(k * 128, (k + 1) * 128)
            out_s[k, pl.ds(r, CP, stride=PITCH), :] = out[:, part] + vec_s[3] + field[r + 1, 1, :, part]
            b = hat[:, part] * vec_s[1]
            s = scaled_s[u, :, part]
            one = col_sum(b) * (stds[k] * (1.0 / chans))
            two = col_sum(b * s) * (stds[k] * (1.0 / chans))
            depth[r, :, part] = b * stds[k] - one - s * two

    def step(i, _):
        stds = [front(i * UNROLL + u, u) for u in range(UNROLL)]
        for u in range(UNROLL):
            middle(u)
        for u in range(UNROLL):
            rear(i * UNROLL + u, u, stds[u])
        g2_s[...] += sum(lax.dot_general(hid_s[u], cotb_s[u], nt, preferred_element_type=f32) for u in range(UNROLL))
        g1_s[...] += sum(lax.dot_general(bp_s[u], norm_s[u], nt, preferred_element_type=f32) for u in range(UNROLL))
        return 0

    lax.fori_loop(0, rows // UNROLL, step, 0)

    def back(c, _):
        x = jnp.concatenate([out_s[k, pl.ds(pl.multiple_of(c * PITCH, 8), rows), :] for k in range(lanes)], axis=1)
        out_ref[c] = x.astype(bf16)
        return 0

    lax.fori_loop(0, chans, back, 0, unroll=2)

    def kernel_chunk(i, _):
        c = pl.multiple_of(i * 8, 8)

        def grad_row(r):
            return tuple(depth[r, pl.ds(c, 8), k * 128 : (k + 1) * 128] for k in range(lanes))

        def fold(acc, a, b, views):
            new = list(acc)
            for s in range(3):
                m = b[0] * views[s][0]
                for k in range(1, lanes):
                    m = m + b[k] * views[s][k]
                new[3 * a + s] = new[3 * a + s] + m
            return tuple(new)

        acc = tuple(jnp.zeros((8, 128), f32) for _ in range(9))
        b0 = grad_row(0)
        acc = fold(acc, 0, b0, shifted(0, c))
        b1 = grad_row(1)
        v = shifted(1, c)
        acc = fold(fold(acc, 0, b1, v), 1, b0, v)

        def go(r, carry):
            acc, b1, b0 = carry
            v = shifted(r, c)
            b = grad_row(r)
            acc = fold(fold(fold(acc, 0, b, v), 1, b1, v), 2, b0, v)
            return acc, b, b1

        acc, b1, b0 = lax.fori_loop(2, rows, go, (acc, b1, b0), unroll=3)
        v = shifted(rows, c)
        acc = fold(fold(acc, 1, b1, v), 2, b0, v)
        acc = fold(acc, 2, b1, shifted(rows + 1, c))
        for tap in range(9):
            gk_s[tap, pl.ds(c, 8), :] = acc[tap]
        return 0

    lax.fori_loop(0, CP // 8, kernel_chunk, 0)
    grad_ref[360:384, :] = jnp.zeros((24, 128), f32)
    grad_ref[744:768, :] = jnp.zeros((24, 128), f32)
    grad_ref[0:hidden, 0:CP] = g2_s[0:hidden, :] * scale
    grad_ref[384 : 384 + hidden, 0:CP] = g1_s[0:hidden, :] * scale
    ones = jnp.ones((8, 128), f32)
    for tap in range(9):
        line = lax.dot_general(ones, gk_s[tap], nt, preferred_element_type=f32, precision=lax.Precision.HIGHEST)
        grad_ref[368 + tap : 369 + tap, 0:CP] = line[0:1, :] * scale


def strip_call(blocks, rows, cols, cot, w_in, b_in, kernel, ln_gain, ln_bias, w_one, b_one, w_two, b_two, scale):
    chans, nrow, width = cot.shape
    f32, bf16 = jnp.float32, jnp.bfloat16
    lanes = width // 128
    act = bf16 if HID == 16 else f32
    vm = pl.BlockSpec(memory_space=pltpu.VMEM)
    mem = pltpu.VMEM
    return pl.pallas_call(
        functools.partial(strip_kernel, scale=scale),
        out_shape=(jax.ShapeDtypeStruct((chans, nrow, width), bf16), jax.ShapeDtypeStruct((768, 128), f32)),
        in_specs=[vm] * 13,
        out_specs=(vm, vm),
        scratch_shapes=[
            mem((nrow + 2, 3, CP, width), f32),
            mem((2, CP, 128), f32),
            mem((nrow, CP, width), f32),
            mem((lanes, CP * PITCH + PITCH, 128), f32),
            mem((lanes, CP * PITCH + PITCH, 128), f32),
            mem((UNROLL, CP, width), f32),
            mem((UNROLL, CP, width), bf16),
            mem((UNROLL, CP, width), bf16),
            mem((UNROLL, HP, width), act),
            mem((UNROLL, HP, width), act),
            mem((UNROLL, HP, width), bf16),
            mem((UNROLL, HP, width), bf16),
            mem((HP, CP), f32),
            mem((HP, CP), f32),
            mem((9, CP, 128), f32),
            mem((16, 128), f32),
            mem((13, CP, 128), f32),
            mem((128, 384), f32),
            mem((CP, 16), bf16),
            mem((HP, CP), bf16),
            mem((CP, HP), bf16),
            mem((CP, HP), bf16),
            mem((HP, CP), bf16),
        ],
        compiler_params=pltpu.CompilerParams(vmem_limit_bytes=60 * MIB),
    )(
        blocks, rows, cols, cot, w_in, b_in[None], kernel, ln_gain[None], ln_bias[None], w_one, b_one[None],
        w_two.T, b_two[None],
    )


MESH = pl.DeviceIdType.MESH
MIB = 1024 * 1024
VMEM_BYTES = 60 * MIB
VM = pl.BlockSpec(memory_space=pltpu.VMEM)
SM = pl.BlockSpec(memory_space=pltpu.SMEM)
AXES = ("face", "tile")


def remap_kernel(
    faces, tiles, pick_ref, link_ref, entry_ref, nested_ref, source_ref, weight_ref, placed_ref, rows_ref, cols_ref, weight,
    part, box, got, table, block_of, nest_of, wide_s, narrow_s, box2, got2, edge, upper, lower, packet, packets, ends,
    line, wins, lots, chosen, windows, whole, ids, slot_v, slot_s, send_w, send_s, send_1, recv_1, local, send_2, recv_2, send_ia, recv_ia, send_ib, recv_ib,
    send_v, recv_v, send_p, recv_p, send_e, recv_e, send_n, recv_n, send_l, recv_l,
):
    f32, bf16 = jnp.float32, jnp.bfloat16
    face = lax.axis_index("face")
    tile = lax.axis_index("tile")
    count = faces * tiles
    me = face * tiles + tile
    chans = source_ref.shape[1]
    nrow = count // 4
    loads = weight_ref.shape[0] // 4

    def load(k):
        span = pl.ds(k * loads, loads)
        return pltpu.make_async_copy(weight_ref.at[span], weight.at[span], send_w.at[k])

    for k in range(4):
        load(k).start()
    barrier = pltpu.get_barrier_semaphore()

    def greet(k, _):
        peer = lax.rem(me + k, count)
        pl.semaphore_signal(barrier, inc=1, device_id=(peer // tiles, lax.rem(peer, tiles)), device_id_type=MESH)
        return 0

    lax.fori_loop(1, count, greet, 0)

    row = lax.broadcasted_iota(jnp.int32, (count, count), 0)
    col = lax.broadcasted_iota(jnp.int32, (count, count), 1)

    def turned(v):
        return jnp.broadcast_to(v, (count, count)).T

    ids[0:1, :] = entry_ref[...]
    ids[1:2, :] = nested_ref[...]
    hit = (jnp.broadcast_to(entry_ref[...], (count, count)) >> 7) == row
    fcol = col.astype(f32)
    low = turned(jnp.min(jnp.where(hit, fcol, float(count - 1)), axis=1, keepdims=True))
    high = turned(jnp.max(jnp.where(hit, fcol, 0.0), axis=1, keepdims=True))
    slot_v[...] = jnp.where(row[0:8] == 0, low[0:8], high[0:8]).astype(jnp.int32)
    to_scalars = pltpu.make_async_copy(slot_v, slot_s, send_s)
    to_scalars.start()

    group = 8
    for k in range(4):
        load(k).wait()

        def multiply(i, _):
            for j in range(group):
                e = k * loads + i * group + j
                x = jnp.dot(source_ref[pick_ref[e]], weight[e], preferred_element_type=f32)
                part[e] = x.astype(bf16)
            return 0

        lax.fori_loop(0, loads // group, multiply, 0)

    to_scalars.wait()

    def fill(d, _):
        box[d, 0:16, :] = part[slot_s[0, d] & (count - 1)]
        box[d, 16:32, :] = part[slot_s[1, d] & (count - 1)]
        return 0

    lax.fori_loop(0, count, fill, 0, unroll=8)
    table[face, tile] = ids[...]
    pl.semaphore_wait(barrier, count - 1)

    index = []
    for k in range(1, tiles):
        index.append(
            pltpu.make_async_remote_copy(
                src_ref=ids,
                dst_ref=table.at[face, tile],
                send_sem=send_ia.at[k],
                recv_sem=recv_ia.at[k],
                device_id=(face, lax.rem(tile + k, tiles)),
                device_id_type=MESH,
            )
        )
        index[-1].start()

    def exchange(src, dst, send, recv):
        def push(k, _):
            peer = lax.rem(me + k, count)
            pltpu.make_async_remote_copy(
                src_ref=src.at[peer],
                dst_ref=dst.at[me],
                send_sem=send,
                recv_sem=recv,
                device_id=(peer // tiles, lax.rem(peer, tiles)),
                device_id_type=MESH,
            ).start()
            return 0

        lax.fori_loop(1, count, push, 0, unroll=2)
        own = pltpu.make_async_copy(src.at[me], dst.at[me], local)
        own.start()
        return own

    def arrive(own, src, dst, recv):
        whole_box = pl.ds(0, count - 1)
        own.wait()
        pltpu.make_async_copy(src.at[whole_box], dst.at[whole_box], recv).wait()

    own = exchange(box, got, send_1, recv_1)
    for copy in index:
        copy.wait()
    index = []
    for k in range(1, faces):
        index.append(
            pltpu.make_async_remote_copy(
                src_ref=table.at[face],
                dst_ref=table.at[face],
                send_sem=send_ib.at[k],
                recv_sem=recv_ib.at[k],
                device_id=(lax.rem(face + k, faces), tile),
                device_id_type=MESH,
            )
        )
        index[-1].start()
    for copy in index:
        copy.wait()

    def spread(f, _):
        for t in range(tiles):
            pair = table[f, t]
            block_of[pl.ds(f * tiles + t, 1), :] = pair[0:1, :]
            nest_of[pl.ds(f * tiles + t, 1), :] = pair[1:2, :]
        return 0

    lax.fori_loop(0, faces, spread, 0)
    blocks = block_of[...]
    hit = (blocks >> 7) == me
    key = (col * count + (blocks & (count - 1))).astype(f32)
    low = jnp.min(jnp.where(hit, key, 1e9), axis=1, keepdims=True)
    high = jnp.max(jnp.where(hit, key, -1.0), axis=1, keepdims=True)
    low_label = jnp.where(high >= 0.0, low.astype(jnp.int32) & (count - 1), -1).astype(f32)
    high_label = jnp.where(high > low, high.astype(jnp.int32) & (count - 1), -1).astype(f32)
    nest = jnp.broadcast_to(nested_ref[...], (count, count))
    perm = jnp.sum(jnp.where((nest >> 7) == row, col.astype(f32), 0.0), axis=1, keepdims=True)
    take_low = (turned(low_label) == perm).astype(f32).astype(bf16)
    take_high = (turned(high_label) == perm).astype(f32).astype(bf16)
    nest = nest_of[...]
    spot = jnp.sum(jnp.where((nest >> 7) == me, (nest & (count - 1)).astype(f32), 0.0), axis=1, keepdims=True)
    place = (turned(spot) == row.astype(f32)).astype(f32).astype(bf16)

    arrive(own, box, got, recv_1)
    deep = 40

    def widen(s, _):
        wide_s[pl.ds(pl.multiple_of(s * deep, 8), 32), :] = got[s].astype(f32)
        return 0

    lax.fori_loop(0, count, widen, 0, unroll=8)
    pitch = 24
    for c in range(chans):
        one = wide_s[pl.ds(c, count, stride=deep), :].astype(bf16)
        two = wide_s[pl.ds(16 + c, count, stride=deep), :].astype(bf16)
        y = jnp.dot(take_low, one, preferred_element_type=f32) + jnp.dot(take_high, two, preferred_element_type=f32)
        narrow_s[pl.ds(c, count, stride=pitch), :] = y

    def narrow(d, _):
        box2[d] = narrow_s[pl.ds(pl.multiple_of(d * pitch, 8), 16), :].astype(bf16)
        return 0

    lax.fori_loop(0, count, narrow, 0, unroll=8)
    own = exchange(box2, got2, send_2, recv_2)
    arrive(own, box2, got2, recv_2)

    def widen_two(s, _):
        wide_s[pl.ds(pl.multiple_of(s * pitch, 8), 16), :] = got2[s].astype(f32)
        return 0

    lax.fori_loop(0, count, widen_two, 0, unroll=8)
    for c in range(chans):
        one = wide_s[pl.ds(c, count, stride=pitch), :].astype(bf16)
        narrow_s[pl.ds(c, count, stride=pitch), :] = jnp.dot(place, one, preferred_element_type=f32)

    def settle(m, _):
        placed_ref[m] = narrow_s[pl.ds(pl.multiple_of(m * pitch, 8), 16), :].astype(bf16)
        return 0

    lax.fori_loop(0, count, settle, 0, unroll=8)

    for k in range(4):
        edge[0, k] = placed_ref[k]
        edge[1, k] = placed_ref[4 * nrow - 4 + k]
    down = lax.rem(tile + 1, tiles)
    up = lax.rem(tile + tiles - 1, tiles)
    vertical = []
    for k, (dst, peer) in enumerate(((upper, down), (lower, up))):
        vertical.append(
            pltpu.make_async_remote_copy(
                src_ref=edge.at[1 - k],
                dst_ref=dst,
                send_sem=send_v.at[k],
                recv_sem=recv_v.at[k],
                device_id=(face, peer),
                device_id_type=MESH,
            )
        )
        vertical[-1].start()

    def end_copy(k, side):
        return pltpu.make_async_remote_copy(
            src_ref=edge.at[side],
            dst_ref=ends.at[side],
            send_sem=send_e.at[k],
            recv_sem=recv_e.at[side],
            device_id=(face, lax.rem(tile + k, tiles)),
            device_id_type=MESH,
        )

    for side, owner in ((0, 0), (1, tiles - 1)):

        @pl.when(tile == owner)
        def _():
            for k in range(1, tiles):
                end_copy(k, side).start()
            ends[side] = edge[side]

    lane = lax.broadcasted_iota(jnp.int32, (chans, 128), 1)

    def pick(r, acc):
        left = pltpu.roll(placed_ref[4 * r].astype(f32), r, 1)
        right = pltpu.roll(placed_ref[4 * r + 3].astype(f32), r + nrow + 1, 1)
        return jnp.where(lane == r, left, jnp.where(lane == r + nrow, right, acc))

    packet[...] = lax.fori_loop(0, nrow, pick, jnp.zeros((chans, 128), f32), unroll=8).astype(bf16)
    packets[tile] = packet[...]
    sends = []
    for k in range(1, tiles):
        sends.append(
            pltpu.make_async_remote_copy(
                src_ref=packet,
                dst_ref=packets.at[tile],
                send_sem=send_p.at[k],
                recv_sem=recv_p.at[k],
                device_id=(face, lax.rem(tile + k, tiles)),
                device_id_type=MESH,
            )
        )
        sends[-1].start()
    for copy in sends:
        copy.wait()
    for side, owner in ((0, 0), (1, tiles - 1)):

        @pl.when(tile == owner)
        def _():
            for k in range(1, tiles):
                end_copy(k, side).wait_send()

        @pl.when(tile != owner)
        def _():
            end_copy(1, side).wait_recv()

    per = 128 // nrow
    for side in range(2):
        line[side] = jnp.concatenate([ends[side, k] for k in range(4)], axis=1).astype(f32)
        parts = []
        for block in range(tiles // per):
            acc = jnp.zeros((chans, 128), f32)
            for i in range(per):
                seg = packets[block * per + i].astype(f32)
                seg = pltpu.roll(seg, (128 + (i - side) * nrow) % 128, 1) if i != side else seg
                acc = jnp.where((lane >= i * nrow) & (lane < (i + 1) * nrow), seg, acc)
            parts.append(acc)
        line[2 + side] = jnp.concatenate(parts, axis=1)
    width = tiles * nrow
    for s in range(4):
        full = line[s]
        for k in range(4):
            lots[s, k] = full[:, k * 128 : (k + 1) * 128].astype(bf16)
        near = pltpu.roll(full, lax.rem(width + 1 - tile * nrow, width), 1)[:, 0:128]
        far = pltpu.roll(full, lax.rem(width + 65 - (tiles - 1 - tile) * nrow, width), 1)[:, 0:128]
        wins[s] = jnp.where(lane < 64, near, far).astype(bf16)
    windows[face] = wins[...]
    sends = []
    for k in range(1, faces):
        sends.append(
            pltpu.make_async_remote_copy(
                src_ref=wins,
                dst_ref=windows.at[face],
                send_sem=send_n.at[k],
                recv_sem=recv_n.at[k],
                device_id=(lax.rem(face + k, faces), tile),
                device_id_type=MESH,
            )
        )
        sends[-1].start()

    def lot_copy(k):
        peer = lax.rem(face + k, faces)
        return pltpu.make_async_remote_copy(
            src_ref=chosen.at[k],
            dst_ref=whole.at[face],
            send_sem=send_l.at[k],
            recv_sem=recv_l.at[k],
            device_id=(peer, tile),
            device_id_type=MESH,
        )

    at_end = (tile == 0) | (tile == tiles - 1)
    end_side = jnp.where(tile == 0, 0, 1)

    @pl.when(at_end)
    def _():
        for k in range(1, faces):
            chosen[k] = lots[link_ref[lax.rem(face + k, faces), end_side, 1]]
            lot_copy(k).start()

    for copy in vertical:
        copy.wait()
    for copy in sends:
        copy.wait()
    for side in range(2):
        view = windows[link_ref[face, 2 + side, 0], link_ref[face, 2 + side, 1]]
        spot = jnp.where(link_ref[face, 2 + side, 2] == 1, 65 + nrow - col, col)
        turn = (row == spot).astype(bf16)
        cols_ref[side] = jnp.dot(view, turn, preferred_element_type=f32).astype(bf16)
        rows_ref[side] = (upper, lower)[side][...]

    @pl.when(at_end)
    def _():
        for k in range(1, faces):
            lot_copy(k).wait()

    for side, owner in ((0, 0), (1, tiles - 1)):

        @pl.when(tile == owner)
        def _():
            flip = link_ref[face, side, 2] == 1
            turn = (row == jnp.where(flip, 127 - col, col)).astype(bf16)
            for k in range(4):
                view = whole[link_ref[face, side, 0], jnp.where(flip, 3 - k, k)]
                rows_ref[side, k] = jnp.dot(view, turn, preferred_element_type=f32).astype(bf16)
    whole_box = pl.ds(0, count - 1)
    pltpu.make_async_copy(box.at[whole_box], got.at[whole_box], send_1).wait()
    pltpu.make_async_copy(box2.at[whole_box], got2.at[whole_box], send_2).wait()


def remap_call(pick, links, entries, nested, source, weight, collective_id):
    faces, tiles = lax.axis_size("face"), lax.axis_size("tile")
    count = faces * tiles
    dma = pltpu.SemaphoreType.DMA
    f32, bf16 = jnp.float32, jnp.bfloat16
    mem = pltpu.VMEM
    chans = source.shape[1]
    block = (4, chans, 128)
    return pl.pallas_call(
        functools.partial(remap_kernel, faces, tiles),
        out_shape=(
            jax.ShapeDtypeStruct((count, chans, 128), bf16),
            jax.ShapeDtypeStruct((2,) + block, bf16),
            jax.ShapeDtypeStruct((2, chans, 128), bf16),
        ),
        in_specs=[SM, SM, VM, VM, VM, pl.BlockSpec(memory_space=pltpu.HBM)],
        out_specs=(VM, VM, VM),
        scratch_shapes=[
            mem(weight.shape, bf16),
            mem((count, chans, 128), bf16),
            mem((count, 32, 128), bf16),
            mem((count, 32, 128), bf16),
            mem((faces, tiles, 2, 128), jnp.int32),
            mem((count, 128), jnp.int32),
            mem((count, 128), jnp.int32),
            mem((count * 40 + 40, 128), f32),
            mem((count * 24 + 24, 128), f32),
            mem((count, chans, 128), bf16),
            mem((count, chans, 128), bf16),
            mem((2,) + block, bf16),
            mem(block, bf16),
            mem(block, bf16),
            mem((chans, 128), bf16),
            mem((tiles, chans, 128), bf16),
            mem((2,) + block, bf16),
            mem((4, chans, 512), f32),
            mem(block, bf16),
            mem((4,) + block, bf16),
            mem((faces,) + block, bf16),
            mem((faces,) + block, bf16),
            mem((faces,) + block, bf16),
            mem((2, 128), jnp.int32),
            mem((8, 128), jnp.int32),
            pltpu.SMEM((8, 128), jnp.int32),
            dma((4,)),
            dma, dma, dma, dma, dma, dma,
            dma((tiles,)), dma((tiles,)), dma((faces,)), dma((faces,)),
            dma((2,)), dma((2,)), dma((tiles,)), dma((tiles,)), dma((tiles,)), dma((2,)), dma((faces,)), dma((faces,)),
            dma((faces,)), dma((faces,)),
        ],
        compiler_params=pltpu.CompilerParams(
            collective_id=collective_id, has_side_effects=True, vmem_limit_bytes=VMEM_BYTES
        ),
    )(pick, links, entries, nested, source, weight)


def reduce_kernel(
    faces, tiles, wide_ref, one_ref, two_ref, ker_ref, grad_ref, first, part, second, mine, full, send_a, recv_a, send_b, recv_b,
    send_c, recv_c,
):
    face = lax.axis_index("face")
    tile = lax.axis_index("tile")
    f32, bf16 = jnp.float32, jnp.bfloat16
    size = wide_ref.shape[0] // tiles
    barrier = pltpu.get_barrier_semaphore()
    for k in range(1, tiles):
        pl.semaphore_signal(barrier, inc=1, device_id=(face, lax.rem(tile + k, tiles)), device_id_type=MESH)
    for k in range(1, faces):
        pl.semaphore_signal(barrier, inc=1, device_id=(lax.rem(face + k, faces), tile), device_id_type=MESH)
    grad_ref[...] = wide_ref[...].astype(bf16)
    pl.semaphore_wait(barrier, tiles + faces - 2)

    def spot(t):
        return pl.ds(pl.multiple_of(t * size, 16), size)

    copies = []
    for k in range(1, tiles):
        peer = lax.rem(tile + k, tiles)
        copies.append(
            pltpu.make_async_remote_copy(
                src_ref=grad_ref.at[spot(peer)],
                dst_ref=first.at[k],
                send_sem=send_a.at[k],
                recv_sem=recv_a.at[k],
                device_id=(face, peer),
                device_id_type=MESH,
            )
        )
        copies[-1].start()
    total = wide_ref[spot(tile), :]
    for k in range(1, tiles):
        copies[k - 1].wait_recv()
        total = total + first[k].astype(f32)
    part[...] = total.astype(bf16)
    second[face] = part[...]
    later = []
    for k in range(1, faces):
        later.append(
            pltpu.make_async_remote_copy(
                src_ref=part,
                dst_ref=second.at[face],
                send_sem=send_b.at[k],
                recv_sem=recv_b.at[k],
                device_id=(lax.rem(face + k, faces), tile),
                device_id_type=MESH,
            )
        )
        later[-1].start()
    for copy in later:
        copy.wait_recv()
    total = second[0].astype(f32)
    for k in range(1, faces):
        total = total + second[k].astype(f32)
    mine[...] = total.astype(bf16)
    full[spot(tile), :] = mine[...]
    last = []
    for k in range(1, tiles):
        last.append(
            pltpu.make_async_remote_copy(
                src_ref=mine,
                dst_ref=full.at[spot(tile)],
                send_sem=send_c.at[k],
                recv_sem=recv_c.at[k],
                device_id=(face, lax.rem(tile + k, tiles)),
                device_id_type=MESH,
            )
        )
        last[-1].start()
    for copy in last:
        copy.wait_recv()
    two_ref[...] = full[0:384, :].astype(f32).T[0:90, 0:360]
    one_ref[...] = full[384:768, :].astype(f32).T[0:90, 0:360]
    ker_ref[...] = full[368:384, 0:90].astype(f32)[0:9]
    for copy in copies + later + last:
        copy.wait_send()


def reduce_call(grad, collective_id):
    faces, tiles = lax.axis_size("face"), lax.axis_size("tile")
    dma = pltpu.SemaphoreType.DMA
    f32, bf16 = jnp.float32, jnp.bfloat16
    size = grad.shape[0] // tiles
    return pl.pallas_call(
        functools.partial(reduce_kernel, faces, tiles),
        out_shape=(
            jax.ShapeDtypeStruct((90, 360), f32),
            jax.ShapeDtypeStruct((90, 360), f32),
            jax.ShapeDtypeStruct((9, 90), f32),
        ),
        in_specs=[VM],
        out_specs=(VM, VM, VM),
        scratch_shapes=[
            pltpu.VMEM(grad.shape, bf16),
            pltpu.VMEM((tiles, size, 128), bf16),
            pltpu.VMEM((size, 128), bf16),
            pltpu.VMEM((faces, size, 128), bf16),
            pltpu.VMEM((size, 128), bf16),
            pltpu.VMEM(grad.shape, bf16),
            dma((tiles,)), dma((tiles,)), dma((faces,)), dma((faces,)), dma((tiles,)), dma((tiles,)),
        ],
        compiler_params=pltpu.CompilerParams(
            collective_id=collective_id, has_side_effects=True, vmem_limit_bytes=24 * MIB
        ),
    )(grad)


def remap(source, entry_block, entry_source, entry_weight, lat_to_nested, face_links):
    return remap_call(entry_source, face_links, entry_block[None], lat_to_nested[None], source, entry_weight, 1)

def per_device(
    source, entry_block, entry_source, entry_weight, lat_to_nested, face_links, w_in, b_in, kernel, ln_gain, ln_bias,
    w_one, b_one, w_two, b_two, cotangent,
):
    face_count = lax.axis_size("face")
    width = cotangent.shape[3]
    box, rows, cols = remap(source, entry_block, entry_source, entry_weight, lat_to_nested, face_links)
    scale = 1.0 / math.sqrt(face_count * width * width)
    output, grad = strip_call(
        box, rows, cols, cotangent[0], w_in, b_in, kernel, ln_gain, ln_bias, w_one, b_one, w_two, b_two,
        scale,
    )
    grad_one, grad_two, grad_kernel = reduce_call(grad, 4)
    return (output[None], grad_one, grad_two.T, grad_kernel)


def solution(mesh):
    split = P(("face", "tile"))
    strips = P("face", None, "tile", None)
    return jax.shard_map(
        per_device,
        mesh=mesh,
        in_specs=(split,) * 5 + (P(),) * 10 + (strips,),
        out_specs=(strips, P(), P(), P()),
        check_vma=False,
    )
```

time: 156 us -> 127 us (0.81)
  Pallas kernels: 139 us -> 120 us
  local copies, waits for them, and re-layouts: 12.4 us -> 5.55 us
  other arithmetic: 3.22 us -> 0 us
    pallas_call x5 -> x1, Pallas kernels: 65.2 us -> 52.6 us  [remap_call(): pl.pallas_call(functools.partial(remap_kernel, faces, tiles), out_shape=(...]
    unnamed x21 -> x6, local copies, waits for them, and re-layouts: 10.5 us -> 4.3 us
    pallas_call x1, Pallas kernels: 26.9 us -> 20.9 us  [reduce_call(): pl.pallas_call(functools.partial(reduce_kernel, faces, tiles), out_shape=...]
where the time goes in v3:
time: 127 us; the launch traced here: 126 us
  Pallas kernels  120 us (94%)
  local copies, waits for them, and re-layouts  5.55 us (4%)
    pallas_call x1, Pallas kernels, remap_call(): pl.pallas_call(functools.partial(remap_kernel, faces, tiles), out_shape=(...  52.6 us
    pallas_call x1, Pallas kernels, strip_call(): pl.pallas_call(functools.partial(strip_kernel, scale=scale), out_shape=(j...  46.6 us
    pallas_call x1, Pallas kernels, reduce_call(): pl.pallas_call(functools.partial(reduce_kernel, faces, tiles), out_shape=...  20.9 us
    unnamed x6, local copies, waits for them, and re-layouts  4.3 us

profile of v3, /device:TPU:1, one launch (start us, length us, event | category | flops | bytes accessed | tf_op | source)
XLA Modules:
  0.0 126.4 jit_solution(9763041978256431731)
XLA Ops:
  0.6 1.2 broadcast_in_dim.29.bone_ref
  1.9 1.4 %copy.20.link_ref = s32[8,4,3]{2,1,0:T(4,128)} copy(s32[8,4,3]{0,1,2:T(4,128)} %param.21) | data formatting | bytes 768 | tf_op args[5]
  3.3 52.6 %shard_map.183 = (bf16[128,16,128]{2,1,0:T(8,128)(2,1)}, bf16[2,4,16,128]{3,2,1,0:T(8,128)(2,1)}, bf16[2,16,128]{2,1,0:T(8,128)(2,1)}) custom-call(s32[128]{0:T(128)} %pick_ref.1, s32[8,4,3]{2,1,0:T(4,128)} %copy.20.link_ref, s32[1,128]{1,0:T(1,128)} %bitcast.17, s32[1,128]{1,0:T(1,128)} %bitcast.18, bf16[64,16,128]{2,1,0:T(8,128)(2,1)} %source_ref.1, ...), custom_call_target="tpu_custom_call" | custom-call | tf_op jit(solution)/shard_map/pallas_call | solution.py:653
  55.9 46.6 %shard_map.184 = (bf16[90,32,512]{2,1,0:T(8,128)(2,1)}, f32[768,128]{1,0:T(8,128)}) custom-call(bf16[128,16,128]{2,1,0:T(8,128)(2,1)} %get-tuple-element.12.blocks_ref, bf16[2,4,16,128]{3,2,1,0:T(8,128)(2,1)} %get-tuple-element.13.rows_ref, bf16[2,16,128]{2,1,0:T(8,128)(2,1)} %get-tuple-element.14.cols_ref, bf16[90,32,512]{2,1,0:T(8,128)(2,1)} %bitcast.11, ...), custom_call_target="tpu_custom_call" | custom-call | tf_op jit(solution)/shard_map/pallas_call | solution.py:256
  102.5 0.0 copy-start
  102.5 1.0 copy-done
  103.5 20.9 %shard_map.185 = (f32[90,360]{1,0:T(8,128)S(1)}, f32[90,360]{1,0:T(8,128)S(1)}, f32[9,90]{1,0:T(8,128)S(1)}) custom-call(f32[768,128]{1,0:T(8,128)S(1)} %copy-done), custom_call_target="tpu_custom_call" | custom-call | tf_op jit(solution)/shard_map/pallas_call | solution.py:787
  124.5 0.7 copy.24
  125.1 0.7 copy.25
  125.8 0.6 copy.26
Async XLA Ops:
  102.5 1.0 copy-start

commit v4 on v3

--- a/solution.py
+++ b/solution.py
@@ -15,15 +15,15 @@
 CP = 96
 HP = 368
 PITCH = 40
-UNROLL = 2
-HID = 16
+SLOTS = 4
 MIB = 1024 * 1024
 
 
 def strip_kernel(
     blocks_ref, rows_ref, cols_ref, cot_ref, win_ref, bin_ref, ker_ref, gain_ref, bias_ref, wone_ref,
-    bone_ref, wtwo_ref, btwo_ref, out_ref, grad_ref, field, cols, depth, cot_s, out_s, scaled_s, norm_s, cotb_s,
-    pre_s, back_s, hid_s, bp_s, g2_s, g1_s, gk_s, tab_s, vec_s, flat_s, w_in_s, w1t_s, w1_s, w2t_s, w2_s, scale,
+    bone_ref, wtwo_ref, btwo_ref, out_ref, grad_ref, cot_v, out_v, field, cols, depth, back_d, turn_s, cot_t, out_t,
+    scaled_s, norm_s, stds_s, pre_s, back_s, hid_s, bp_s, raw_s, g2_s, g1_s, gk_s, tab_s, vec_s, flat_s, w_in_s, w1t_s,
+    w1_s, w2t_s, w2_s, sem_in, sem_out, scale,
 ):
     chans, rows, width = cot_ref.shape
     hidden = wone_ref.shape[1]
@@ -33,6 +33,9 @@
 
     def wide(v):
         return jnp.concatenate([v] * lanes, axis=1)
+
+    bring = pltpu.make_async_copy(cot_ref, cot_v, sem_in)
+    bring.start()
 
     tab_s[...] = jnp.zeros_like(tab_s)
     for j, ref in enumerate((bin_ref, gain_ref, bias_ref, btwo_ref)):
@@ -47,9 +50,10 @@
     flat_s[...] = jnp.zeros_like(flat_s)
     flat_s[0:chans, 0:hidden] = wone_ref[...].astype(f32)
     w1_s[...] = flat_s[0:CP, 0:HP].astype(bf16)
-    high = bone_ref[...].astype(bf16).astype(f32)
+    bone = bone_ref[0:1, 0:hidden]
+    high = bone.astype(bf16).astype(f32)
     flat_s[chans : chans + 1, 0:hidden] = high
-    flat_s[chans + 1 : chans + 2, 0:hidden] = bone_ref[...] - high
+    flat_s[chans + 1 : chans + 2, 0:hidden] = bone - high
     w1t_s[...] = (flat_s[...].T[0:HP, 0:CP] * 0.5).astype(bf16)
     flat_s[...] = jnp.zeros_like(flat_s)
     flat_s[0:chans, 0:hidden] = wtwo_ref[...].astype(f32)
@@ -66,16 +70,6 @@
 
     g2_s[...] = jnp.zeros_like(g2_s)
     g1_s[...] = jnp.zeros_like(g1_s)
-    cot_s[:, chans * PITCH :, :] = jnp.zeros((lanes, (CP + 1 - chans) * PITCH, 128), f32)
-
-    def turn(c, _):
-        x = cot_ref[c].astype(f32)
-        for k in range(lanes):
-            cot_s[k, pl.ds(pl.multiple_of(c * PITCH, 8), rows), :] = x[:, k * 128 : (k + 1) * 128]
-        return 0
-
-    lax.fori_loop(0, chans, turn, 0, unroll=2)
-
     def make_row(at, x):
         lat = jnp.dot(w_in_s[...], x, preferred_element_type=f32) + wide(vec_s[0])
         lat = lat.astype(bf16).astype(f32)
@@ -98,6 +92,26 @@
 
     lax.fori_loop(0, rows, row_step, 0, unroll=2)
 
+    bring.wait()
+    turn_s[...] = jnp.zeros_like(turn_s)
+
+    def turn(i, _):
+        for j in range(16):
+            c = i * 16 + j
+
+            @pl.when(c < chans)
+            def _():
+                x = cot_v[c].astype(f32)
+                for k in range(lanes):
+                    turn_s[k, j * PITCH : j * PITCH + rows, :] = x[:, k * 128 : (k + 1) * 128]
+
+        for r in range(rows):
+            x = jnp.concatenate([turn_s[k, pl.ds(r, 16, stride=PITCH), :] for k in range(lanes)], axis=1)
+            cot_t[r, pl.ds(pl.multiple_of(i * 16, 16), 16), :] = x.astype(bf16)
+        return 0
+
+    lax.fori_loop(0, CP // 16, turn, 0)
+
     def shifted(r, c):
         return [
             [field[r, side, pl.ds(c, 8), k * 128 : (k + 1) * 128] for k in range(lanes)] for side in range(3)
@@ -136,73 +150,147 @@
     def col_sum(v):
         return jnp.sum(v, axis=0, keepdims=True)
 
-    def front(r, u):
-        stds = []
-        for k in range(lanes):
+    def norm_units(r, u):
+        def unit(k):
             part = slice(k * 128, (k + 1) * 128)
             d = depth[r, :, part]
             d = d - col_sum(d) * (1.0 / chans)
             d = jnp.where(real, d, 0.0)
             inv_std = lax.rsqrt(col_sum(d * d) * (1.0 / chans) + NORM_EPS)
             s = d * inv_std
-            scaled_s[u, :, part] = s
+            at = lax.rem(r, 8)
+            scaled_s[at, :, part] = s
+            stds_s[at, :, part] = jnp.broadcast_to(inv_std, (8, 128))
             n = jnp.where(ones_rows, 1.0, s * vec_s[1] + vec_s[2])
-            norm_s[u, :, part] = n.astype(bf16)
-            cotb_s[u, :, part] = cot_s[k, pl.ds(r, CP, stride=PITCH), :].astype(bf16)
-            stds.append(inv_std)
-        pre_s[u] = jnp.dot(w1t_s[...], norm_s[u], preferred_element_type=f32).astype(pre_s.dtype)
-        back_s[u] = jnp.dot(w2_s[...], cotb_s[u], preferred_element_type=f32).astype(back_s.dtype)
-        return stds
-
-    def middle(u):
-        ty = pre_s.dtype
-        num = lambda v: jnp.asarray(v, ty)
-        for h in range(0, HP, 16):
-            x = pre_s[u, h : h + 16, :]
+            norm_s[u % 4, :, part] = n.astype(bf16)
+
+        return [functools.partial(unit, k) for k in range(lanes)]
+
+    halves = [slice(n, n + 256) for n in range(0, width, 256)]
+
+    def widen_units(r, u):
+        def pre(part):
+            x = jnp.dot(w1t_s[...], norm_s[u % 4, :, part], preferred_element_type=f32)
+            pre_s[u % 2, :, part] = x.astype(bf16)
+
+        def back(part):
+            x = jnp.dot(w2_s[...], cot_t[r, :, part], preferred_element_type=f32)
+            back_s[u % 2, :, part] = x.astype(bf16)
+
+        return [functools.partial(f, part) for part in halves for f in (pre, back)]
+
+    def gelu_units(r, u):
+        num = lambda v: jnp.asarray(v, bf16)
+
+        def unit(h):
+            x = pre_s[u % 2, h : h + 16, :]
             q = x * x
             t = jnp.tanh(x * (num(2.0 * GELU_K) + num(8.0 * GELU_K * GELU_C) * q))
             p = num(1.0) + t
             g = x * p
             slope = p + g * (num(1.0) - t) * (num(2.0 * GELU_K) + num(24.0 * GELU_K * GELU_C) * q)
-            hid_s[u, h : h + 16, :] = g.astype(bf16)
-            bp_s[u, h : h + 16, :] = (back_s[u, h : h + 16, :] * slope).astype(bf16)
-
-    def rear(r, u, stds):
-        out = jnp.dot(w2t_s[...], hid_s[u], preferred_element_type=f32)
-        hat = jnp.dot(w1_s[...], bp_s[u], preferred_element_type=f32)
-        for k in range(lanes):
+            hid_s[u % 2, h : h + 16, :] = g
+            bp_s[u % 2, h : h + 16, :] = back_s[u % 2, h : h + 16, :] * slope
+
+        return [functools.partial(unit, h) for h in range(0, HP, 16)]
+
+    def narrow_units(r, u):
+        def out(part):
+            raw_s[u % 2, 0, :, part] = jnp.dot(w2t_s[...], hid_s[u % 2, :, part], preferred_element_type=f32)
+
+        def hat(part):
+            raw_s[u % 2, 1, :, part] = jnp.dot(w1_s[...], bp_s[u % 2, :, part], preferred_element_type=f32)
+
+        def two():
+            g2_s[...] += lax.dot_general(hid_s[u % 2], cot_t[r], nt, preferred_element_type=f32)
+
+        def one():
+            g1_s[...] += lax.dot_general(bp_s[u % 2], norm_s[u % 4], nt, preferred_element_type=f32)
+
+        units = [functools.partial(f, part) for part in halves for f in (out, hat)]
+        return [units[0], units[1], two, units[2], units[3], one]
+
+    def rear_units(r, u):
+        def unit(k):
             part = slice(k * 128, (k + 1) * 128)
-            out_s[k, pl.ds(r, CP, stride=PITCH), :] = out[:, part] + vec_s[3] + field[r + 1, 1, :, part]
-            b = hat[:, part] * vec_s[1]
-            s = scaled_s[u, :, part]
-            one = col_sum(b) * (stds[k] * (1.0 / chans))
-            two = col_sum(b * s) * (stds[k] * (1.0 / chans))
-            depth[r, :, part] = b * stds[k] - one - s * two
+            at = lax.rem(r, 8)
+            out_t[r, :, part] = (raw_s[u % 2, 0, :, part] + vec_s[3] + field[r + 1, 1, :, part]).astype(bf16)
+            inv_std = stds_s[at, 0:1, part]
+            b = raw_s[u % 2, 1, :, part] * vec_s[1]
+            s = scaled_s[at, :, part]
+            one = col_sum(b) * (inv_std * (1.0 / chans))
+            two = col_sum(b * s) * (inv_std * (1.0 / chans))
+            back_d[r, :, part] = b * inv_std - one - s * two
+
+        return [functools.partial(unit, k) for k in range(lanes)]
+
+    def beat(at, u, live):
+        units = [
+            make(at - s, u - s) if ok else []
+            for s, (make, ok) in enumerate(zip((norm_units, widen_units, gelu_units, narrow_units, rear_units), live))
+        ]
+        vector = units[2]
+        extra = units[0] + units[4]
+        if extra and vector:
+            gap = max(1, len(vector) // len(extra))
+            mixed = []
+            for i, v in enumerate(vector):
+                mixed.append(v)
+                if i % gap == gap - 1 and extra:
+                    mixed.append(extra.pop(0))
+            vector = mixed + extra
+        else:
+            vector = vector + extra
+        matrix = []
+        for i in range(max(len(units[1]), len(units[3]))):
+            matrix += units[3][i : i + 1] + units[1][i : i + 1]
+        share = len(vector) / max(1, len(matrix))
+        done = 0
+        for i, m in enumerate(matrix):
+            m()
+            upto = round((i + 1) * share)
+            for v in vector[done:upto]:
+                v()
+            done = upto
+        for v in vector[done:]:
+            v()
+
+    for at in range(4):
+        beat(at, at, [at - s >= 0 for s in range(5)])
 
     def step(i, _):
-        stds = [front(i * UNROLL + u, u) for u in range(UNROLL)]
-        for u in range(UNROLL):
-            middle(u)
-        for u in range(UNROLL):
-            rear(i * UNROLL + u, u, stds[u])
-        g2_s[...] += sum(lax.dot_general(hid_s[u], cotb_s[u], nt, preferred_element_type=f32) for u in range(UNROLL))
-        g1_s[...] += sum(lax.dot_general(bp_s[u], norm_s[u], nt, preferred_element_type=f32) for u in range(UNROLL))
-        return 0
-
-    lax.fori_loop(0, rows // UNROLL, step, 0)
-
-    def back(c, _):
-        x = jnp.concatenate([out_s[k, pl.ds(pl.multiple_of(c * PITCH, 8), rows), :] for k in range(lanes)], axis=1)
-        out_ref[c] = x.astype(bf16)
-        return 0
-
-    lax.fori_loop(0, chans, back, 0, unroll=2)
+        for u in range(SLOTS):
+            beat(4 + i * SLOTS + u, 4 + u, [True] * 5)
+        return 0
+
+    lax.fori_loop(0, rows // SLOTS - 1, step, 0)
+    for at in range(rows, rows + 4):
+        beat(at, at, [at - s < rows for s in range(5)])
+
+    def back(i, _):
+        for r in range(rows):
+            x = out_t[r, pl.ds(pl.multiple_of(i * 16, 16), 16), :].astype(f32)
+            for k in range(lanes):
+                turn_s[k, pl.ds(r, 16, stride=PITCH), :] = x[:, k * 128 : (k + 1) * 128]
+        for j in range(16):
+            c = i * 16 + j
+
+            @pl.when(c < chans)
+            def _():
+                x = jnp.concatenate([turn_s[k, j * PITCH : j * PITCH + rows, :] for k in range(lanes)], axis=1)
+                out_v[c] = x.astype(bf16)
+
+        return 0
+
+    lax.fori_loop(0, CP // 16, back, 0)
+    take = pltpu.make_async_copy(out_v, out_ref, sem_out)
+    take.start()
 
     def kernel_chunk(i, _):
         c = pl.multiple_of(i * 8, 8)
 
         def grad_row(r):
-            return tuple(depth[r, pl.ds(c, 8), k * 128 : (k + 1) * 128] for k in range(lanes))
+            return tuple(back_d[r, pl.ds(c, 8), k * 128 : (k + 1) * 128] for k in range(lanes))
 
         def fold(acc, a, b, views):
             new = list(acc)
@@ -244,33 +332,39 @@
     for tap in range(9):
         line = lax.dot_general(ones, gk_s[tap], nt, preferred_element_type=f32, precision=lax.Precision.HIGHEST)
         grad_ref[368 + tap : 369 + tap, 0:CP] = line[0:1, :] * scale
+    take.wait()
 
 
 def strip_call(blocks, rows, cols, cot, w_in, b_in, kernel, ln_gain, ln_bias, w_one, b_one, w_two, b_two, scale):
     chans, nrow, width = cot.shape
     f32, bf16 = jnp.float32, jnp.bfloat16
     lanes = width // 128
-    act = bf16 if HID == 16 else f32
     vm = pl.BlockSpec(memory_space=pltpu.VMEM)
+    hbm = pl.BlockSpec(memory_space=pltpu.HBM)
     mem = pltpu.VMEM
     return pl.pallas_call(
         functools.partial(strip_kernel, scale=scale),
         out_shape=(jax.ShapeDtypeStruct((chans, nrow, width), bf16), jax.ShapeDtypeStruct((768, 128), f32)),
-        in_specs=[vm] * 13,
-        out_specs=(vm, vm),
+        in_specs=[vm] * 3 + [hbm] + [vm] * 9,
+        out_specs=(hbm, vm),
         scratch_shapes=[
+            mem((chans, nrow, width), bf16),
+            mem((chans, nrow, width), bf16),
             mem((nrow + 2, 3, CP, width), f32),
             mem((2, CP, 128), f32),
             mem((nrow, CP, width), f32),
-            mem((lanes, CP * PITCH + PITCH, 128), f32),
-            mem((lanes, CP * PITCH + PITCH, 128), f32),
-            mem((UNROLL, CP, width), f32),
-            mem((UNROLL, CP, width), bf16),
-            mem((UNROLL, CP, width), bf16),
-            mem((UNROLL, HP, width), act),
-            mem((UNROLL, HP, width), act),
-            mem((UNROLL, HP, width), bf16),
-            mem((UNROLL, HP, width), bf16),
+            mem((nrow, CP, width), f32),
+            mem((lanes, 17 * PITCH, 128), f32),
+            mem((nrow, CP, width), bf16),
+            mem((nrow, CP, width), bf16),
+            mem((8, CP, width), f32),
+            mem((4, CP, width), bf16),
+            mem((8, 8, width), f32),
+            mem((2, HP, width), bf16),
+            mem((2, HP, width), bf16),
+            mem((2, HP, width), bf16),
+            mem((2, HP, width), bf16),
+            mem((2, 2, CP, width), f32),
             mem((HP, CP), f32),
             mem((HP, CP), f32),
             mem((9, CP, 128), f32),
@@ -282,10 +376,12 @@
             mem((CP, HP), bf16),
             mem((CP, HP), bf16),
             mem((HP, CP), bf16),
+            pltpu.SemaphoreType.DMA,
+            pltpu.SemaphoreType.DMA,
         ],
         compiler_params=pltpu.CompilerParams(vmem_limit_bytes=60 * MIB),
     )(
-        blocks, rows, cols, cot, w_in, b_in[None], kernel, ln_gain[None], ln_bias[None], w_one, b_one[None],
+        blocks, rows, cols, cot, w_in, b_in[None], kernel, ln_gain[None], ln_bias[None], w_one, jnp.pad(b_one, (0, 512 - b_one.shape[0]))[None],
         w_two.T, b_two[None],
     )
 
@@ -504,24 +600,6 @@
         )
         vertical[-1].start()
 
-    def end_copy(k, side):
-        return pltpu.make_async_remote_copy(
-            src_ref=edge.at[side],
-            dst_ref=ends.at[side],
-            send_sem=send_e.at[k],
-            recv_sem=recv_e.at[side],
-            device_id=(face, lax.rem(tile + k, tiles)),
-            device_id_type=MESH,
-        )
-
-    for side, owner in ((0, 0), (1, tiles - 1)):
-
-        @pl.when(tile == owner)
-        def _():
-            for k in range(1, tiles):
-                end_copy(k, side).start()
-            ends[side] = edge[side]
-
     lane = lax.broadcasted_iota(jnp.int32, (chans, 128), 1)
 
     def pick(r, acc):
@@ -544,6 +622,24 @@
             )
         )
         sends[-1].start()
+    def end_copy(k, side):
+        return pltpu.make_async_remote_copy(
+            src_ref=edge.at[side],
+            dst_ref=ends.at[side],
+            send_sem=send_e.at[k],
+            recv_sem=recv_e.at[side],
+            device_id=(face, lax.rem(tile + k, tiles)),
+            device_id_type=MESH,
+        )
+
+    for side, owner in ((0, 0), (1, tiles - 1)):
+
+        @pl.when(tile == owner)
+        def _():
+            for k in range(1, tiles):
+                end_copy(k, side).start()
+            ends[side] = edge[side]
+
     for copy in sends:
         copy.wait()
     for side, owner in ((0, 0), (1, tiles - 1)):
@@ -572,8 +668,6 @@
     width = tiles * nrow
     for s in range(4):
         full = line[s]
-        for k in range(4):
-            lots[s, k] = full[:, k * 128 : (k + 1) * 128].astype(bf16)
         near = pltpu.roll(full, lax.rem(width + 1 - tile * nrow, width), 1)[:, 0:128]
         far = pltpu.roll(full, lax.rem(width + 65 - (tiles - 1 - tile) * nrow, width), 1)[:, 0:128]
         wins[s] = jnp.where(lane < 64, near, far).astype(bf16)
@@ -608,8 +702,11 @@
 
     @pl.when(at_end)
     def _():
+        for s in range(4):
+            for k in range(4):
+                lots[s, k] = line[s, :, k * 128 : (k + 1) * 128].astype(bf16)
         for k in range(1, faces):
-            chosen[k] = lots[link_ref[lax.rem(face + k, faces), end_side, 1]]
+            chosen[k] = lots[link_ref[1, end_side, lax.rem(face + k, faces)]]
             lot_copy(k).start()
 
     for copy in vertical:
@@ -617,8 +714,8 @@
     for copy in sends:
         copy.wait()
     for side in range(2):
-        view = windows[link_ref[face, 2 + side, 0], link_ref[face, 2 + side, 1]]
-        spot = jnp.where(link_ref[face, 2 + side, 2] == 1, 65 + nrow - col, col)
+        view = windows[link_ref[0, 2 + side, face], link_ref[1, 2 + side, face]]
+        spot = jnp.where(link_ref[2, 2 + side, face] == 1, 65 + nrow - col, col)
         turn = (row == spot).astype(bf16)
         cols_ref[side] = jnp.dot(view, turn, preferred_element_type=f32).astype(bf16)
         rows_ref[side] = (upper, lower)[side][...]
@@ -632,10 +729,10 @@
 
         @pl.when(tile == owner)
         def _():
-            flip = link_ref[face, side, 2] == 1
+            flip = link_ref[2, side, face] == 1
             turn = (row == jnp.where(flip, 127 - col, col)).astype(bf16)
             for k in range(4):
-                view = whole[link_ref[face, side, 0], jnp.where(flip, 3 - k, k)]
+                view = whole[link_ref[0, side, face], jnp.where(flip, 3 - k, k)]
                 rows_ref[side, k] = jnp.dot(view, turn, preferred_element_type=f32).astype(bf16)
     whole_box = pl.ds(0, count - 1)
     pltpu.make_async_copy(box.at[whole_box], got.at[whole_box], send_1).wait()
@@ -809,7 +906,7 @@
 
 
 def remap(source, entry_block, entry_source, entry_weight, lat_to_nested, face_links):
-    return remap_call(entry_source, face_links, entry_block[None], lat_to_nested[None], source, entry_weight, 1)
+    return remap_call(entry_source, face_links.transpose(2, 1, 0), entry_block[None], lat_to_nested[None], source, entry_weight, 1)
 
 def per_device(
     source, entry_block, entry_source, entry_weight, lat_to_nested, face_links, w_in, b_in, kernel, ln_gain, ln_bias,

time: 127 us -> 121 us (0.953)
  Pallas kernels: 120 us -> 116 us
  local copies, waits for them, and re-layouts: 5.55 us -> 4.17 us
    pallas_call x1, Pallas kernels: 46.6 us -> 42.7 us  [strip_call(): pl.pallas_call(functools.partial(strip_kernel, scale=scale), out_shape=(j...]
    unnamed x6 -> x5, local copies, waits for them, and re-layouts: 4.3 us -> 2.91 us
where the time goes in v4:
time: 121 us
  Pallas kernels  116 us (96%)
  local copies, waits for them, and re-layouts  4.17 us (3%)
    pallas_call x1, Pallas kernels, remap_call(): pl.pallas_call(functools.partial(remap_kernel, faces, tiles), out_shape=(...  52.3 us
    pallas_call x1, Pallas kernels, strip_call(): pl.pallas_call(functools.partial(strip_kernel, scale=scale), out_shape=(j...  42.7 us
    pallas_call x1, Pallas kernels, reduce_call(): pl.pallas_call(functools.partial(reduce_kernel, faces, tiles), out_shape=...  21.3 us
    unnamed x5, local copies, waits for them, and re-layouts  2.91 us

profile of v4, /device:TPU:1, one launch (start us, length us, event | category | flops | bytes accessed | tf_op | source)
XLA Modules:
  0.0 121.1 jit_solution(8908364617103426500)
XLA Ops:
  0.6 1.3 %pad.4 = f32[512]{0:T(512)} pad(f32[360]{0:T(512)} %param.28, f32[]{:T(128)} %constant.2.clone.1), padding=0_152 | pad | bytes 3492 | tf_op jit(solution)/shard_map/jit(_pad)/pad | solution.py:384
  1.9 52.3 %shard_map.183 = (bf16[128,16,128]{2,1,0:T(8,128)(2,1)}, bf16[2,4,16,128]{3,2,1,0:T(8,128)(2,1)}, bf16[2,16,128]{2,1,0:T(8,128)(2,1)}) custom-call(s32[128]{0:T(128)} %pick_ref.1, s32[3,4,8]{2,1,0:T(4,128)} %bitcast.16, s32[1,128]{1,0:T(1,128)} %bitcast.17, s32[1,128]{1,0:T(1,128)} %bitcast.18, bf16[64,16,128]{2,1,0:T(8,128)(2,1)} %source_ref.1, ...), custom_call_target="tpu_custom_call" | custom-call | tf_op jit(solution)/shard_map/pallas_call | solution.py:750
  54.2 42.7 %shard_map.184 = (bf16[90,32,512]{2,1,0:T(8,128)(2,1)}, f32[768,128]{1,0:T(8,128)}) custom-call(bf16[128,16,128]{2,1,0:T(8,128)(2,1)} %get-tuple-element.12.blocks_ref, bf16[2,4,16,128]{3,2,1,0:T(8,128)(2,1)} %get-tuple-element.13.rows_ref, bf16[2,16,128]{2,1,0:T(8,128)(2,1)} %get-tuple-element.14.cols_ref, bf16[90,32,512]{2,1,0:T(8,128)(2,1)} %bitcast.13, ...), custom_call_target="tpu_custom_call" | custom-call | tf_op jit(solution)/shard_map/pallas_call | solution.py:345
  96.9 0.0 copy-start
  96.9 1.0 copy-done
  97.8 21.3 %shard_map.185 = (f32[90,360]{1,0:T(8,128)S(1)}, f32[90,360]{1,0:T(8,128)S(1)}, f32[9,90]{1,0:T(8,128)S(1)}) custom-call(f32[768,128]{1,0:T(8,128)S(1)} %copy-done), custom_call_target="tpu_custom_call" | custom-call | tf_op jit(solution)/shard_map/pallas_call | solution.py:884
  119.2 0.7 copy.23
  119.8 0.7 copy.24
  120.5 0.6 copy.25
Async XLA Ops:
  96.9 1.0 copy-start

commit v5 on v4

--- a/solution.py
+++ b/solution.py
@@ -90,7 +90,7 @@
         make_row(r + 1, jnp.concatenate([blocks_ref[r * lanes + k] for k in range(lanes)], axis=1))
         return 0
 
-    lax.fori_loop(0, rows, row_step, 0, unroll=2)
+    lax.fori_loop(0, rows, row_step, 0, unroll=8)
 
     bring.wait()
     turn_s[...] = jnp.zeros_like(turn_s)
@@ -138,7 +138,7 @@
                 tuple(mix(0, v, k) for k in range(lanes)),
             )
 
-        lax.fori_loop(0, rows, go, (one, two), unroll=4)
+        lax.fori_loop(0, rows, go, (one, two), unroll=16)
         return 0
 
     lax.fori_loop(0, CP // 8, conv_chunk, 0)
@@ -315,7 +315,7 @@
             acc = fold(fold(fold(acc, 0, b, v), 1, b1, v), 2, b0, v)
             return acc, b, b1
 
-        acc, b1, b0 = lax.fori_loop(2, rows, go, (acc, b1, b0), unroll=3)
+        acc, b1, b0 = lax.fori_loop(2, rows, go, (acc, b1, b0), unroll=10)
         v = shifted(rows, c)
         acc = fold(fold(acc, 1, b1, v), 2, b0, v)
         acc = fold(acc, 2, b1, shifted(rows + 1, c))

time: 121 us -> 119 us (0.983)
  Pallas kernels: 116 us -> 113 us
    pallas_call x1, Pallas kernels: 42.7 us -> 39.9 us  [strip_call(): pl.pallas_call(functools.partial(strip_kernel, scale=scale), out_shape=(j...]
where the time goes in v5:
time: 119 us; the launch traced here: 118 us
  Pallas kernels  113 us (95%)
  local copies, waits for them, and re-layouts  4.17 us (4%)
    pallas_call x1, Pallas kernels, remap_call(): pl.pallas_call(functools.partial(remap_kernel, faces, tiles), out_shape=(...  52.3 us
    pallas_call x1, Pallas kernels, strip_call(): pl.pallas_call(functools.partial(strip_kernel, scale=scale), out_shape=(j...  39.9 us
    pallas_call x1, Pallas kernels, reduce_call(): pl.pallas_call(functools.partial(reduce_kernel, faces, tiles), out_shape=...  21.3 us
    unnamed x5, local copies, waits for them, and re-layouts  2.91 us

profile of v5, /device:TPU:1, one launch (start us, length us, event | category | flops | bytes accessed | tf_op | source)
XLA Modules:
  0.0 118.3 jit_solution(5781672070551960749)
XLA Ops:
  0.6 1.3 %pad.4 = f32[512]{0:T(512)} pad(f32[360]{0:T(512)} %param.28, f32[]{:T(128)} %constant.2.clone.1), padding=0_152 | pad | bytes 3492 | tf_op jit(solution)/shard_map/jit(_pad)/pad | solution.py:384
  1.9 52.3 %shard_map.183 = (bf16[128,16,128]{2,1,0:T(8,128)(2,1)}, bf16[2,4,16,128]{3,2,1,0:T(8,128)(2,1)}, bf16[2,16,128]{2,1,0:T(8,128)(2,1)}) custom-call(s32[128]{0:T(128)} %pick_ref.1, s32[3,4,8]{2,1,0:T(4,128)} %bitcast.16, s32[1,128]{1,0:T(1,128)} %bitcast.17, s32[1,128]{1,0:T(1,128)} %bitcast.18, bf16[64,16,128]{2,1,0:T(8,128)(2,1)} %source_ref.1, ...), custom_call_target="tpu_custom_call" | custom-call | tf_op jit(solution)/shard_map/pallas_call | solution.py:750
  54.2 39.9 %shard_map.184 = (bf16[90,32,512]{2,1,0:T(8,128)(2,1)}, f32[768,128]{1,0:T(8,128)}) custom-call(bf16[128,16,128]{2,1,0:T(8,128)(2,1)} %get-tuple-element.12.blocks_ref, bf16[2,4,16,128]{3,2,1,0:T(8,128)(2,1)} %get-tuple-element.13.rows_ref, bf16[2,16,128]{2,1,0:T(8,128)(2,1)} %get-tuple-element.14.cols_ref, bf16[90,32,512]{2,1,0:T(8,128)(2,1)} %bitcast.13, ...), custom_call_target="tpu_custom_call" | custom-call | tf_op jit(solution)/shard_map/pallas_call | solution.py:345
  94.1 0.0 copy-start
  94.1 1.0 copy-done
  95.1 21.3 %shard_map.185 = (f32[90,360]{1,0:T(8,128)S(1)}, f32[90,360]{1,0:T(8,128)S(1)}, f32[9,90]{1,0:T(8,128)S(1)}) custom-call(f32[768,128]{1,0:T(8,128)S(1)} %copy-done), custom_call_target="tpu_custom_call" | custom-call | tf_op jit(solution)/shard_map/pallas_call | solution.py:884
  116.4 0.7 copy.23
  117.1 0.7 copy.24
  117.7 0.6 copy.25
Async XLA Ops:
  94.1 1.0 copy-start
